TPU v7x, 32 devices: a whole 2x2x4 slice. The times are simulated.
32 devices in a mesh: layer: 8 (over y, x, core), tile: 4 (over z).
Axes of the slice: x: 2, y: 2, z: 4, core: 2. Of those that a mesh axis runs over, the one named last changes fastest.
Arguments:
- down_tiles: bfloat16 [8, 16, 3, 2, 512, 512], P('layer', 'tile'), may hold values from -0.109375 to 0.109375
- up_tiles: bfloat16 [8, 16, 3, 2, 512, 512], P('layer', 'tile'), may hold values from -0.109375 to 0.109375
- down_source: float32 [8, 2, 32, 8192], P('layer', None, None, 'tile'), may hold values from -3 to 3
- up_source: float32 [8, 2, 32, 8192], P('layer', None, None, 'tile'), may hold values from -3 to 3
- thickness: int32 [8], P('layer'), may hold values from 1 to 2
Outputs:
- field: float32 [8, 2, 32, 8192], P('layer', None, None, 'tile')
All inputs are finite; a program needn't handle non-finite values.
Results may differ from a plain program's by a relative error of at most 0.04.
Values may be sent and summed in bfloat16 or wider, within the bound.
A program may use at most 128 MiB of HBM per device.

v0:
```python
import jax
import jax.numpy as jnp
from jax import lax
from jax.sharding import PartitionSpec as P

COLS = 8


def passed_along(value, axis, steps):
    count = lax.axis_size(axis)
    leading, last = (max(0, -steps), min(count, count - steps))
    return lax.ppermute(value, axis, [(source, source + steps) for source in range(leading, last)])


def extended_2(block, sides, width):
    for axis, dim in sides:
        count = lax.axis_size(axis)
        forward = [(i, i + 1) for i in range(count - 1)]
        backward = [(target, source) for source, target in forward]
        low = lax.ppermute(
            lax.slice_in_dim(block, block.shape[dim] - width, None, axis=dim), axis, forward
        )
        high = lax.ppermute(lax.slice_in_dim(block, 0, width, axis=dim), axis, backward)
        block = jnp.concatenate([low, block, high], axis=dim)
    return block


def combine(inputs, layer_tiles):
    block_rows = layer_tiles.shape[0]
    accum = None
    for offset in range(3):
        partial_value = jnp.einsum(
            "bpct,bqtu->bpqcu",
            inputs[offset : offset + block_rows],
            layer_tiles[:, offset],
            preferred_element_type=jnp.float32,
        )
        accum = partial_value if accum is None else accum + partial_value
    real_part = accum[:, 0, 0] - accum[:, 1, 1]
    imag_part = accum[:, 0, 1] + accum[:, 1, 0]
    return jnp.stack([real_part, imag_part], axis=1)


def shards(down_tiles, up_tiles, down_source, up_source, thickness):
    layer_count = lax.axis_size("layer")
    layer_index = lax.axis_index("layer")
    own_down = down_tiles[0]
    own_up = up_tiles[0]
    block_rows = own_down.shape[0]
    tile_width = own_down.shape[-1]
    batch_count = down_source.shape[2] // COLS
    is_thick = thickness[0] == 2

    def to_blocks(source):
        return source.reshape(2, batch_count, COLS, block_rows, tile_width).transpose(1, 3, 0, 2, 4)

    down_blocks = to_blocks(down_source[0])
    up_blocks = to_blocks(up_source[0])
    trace_shape = (block_rows, 2, COLS, tile_width)

    def zeros_rows(extra):
        return jnp.zeros((block_rows + extra, 2, COLS, tile_width), jnp.float32)

    def both_powers(send_down, send_up, down_live, up_live):
        moved_down = passed_along(send_down, "layer", 1)
        moved_up = passed_along(send_up, "layer", -1)
        received = jnp.stack([moved_down, moved_up], axis=1)
        extended = extended_2(received, (("tile", 0),), 1)
        down_inputs = extended[:, 0]
        up_inputs = extended[:, 1]
        first_down = lax.cond(
            down_live, lambda: combine(down_inputs, own_down), lambda: zeros_rows(0)
        )
        first_up = lax.cond(up_live, lambda: combine(up_inputs, own_up), lambda: zeros_rows(0))
        rim_data = extended_2(
            jnp.stack([first_down, first_up], axis=1).astype(jnp.bfloat16), (("tile", 0),), 1
        )
        second_down = lax.cond(
            down_live & is_thick, lambda: combine(rim_data[:, 0], own_down), lambda: first_down
        )
        second_up = lax.cond(
            up_live & is_thick, lambda: combine(rim_data[:, 1], own_up), lambda: first_up
        )
        return (second_down, second_up)

    def one_step(step_index, state):
        send_down, send_up, out_down, out_up = state
        down_batch = step_index - layer_index
        up_batch = step_index - (layer_count - 1 - layer_index)
        down_live = (down_batch >= 0) & (down_batch < batch_count)
        up_live = (up_batch >= 0) & (up_batch < batch_count)
        down_slot = jnp.clip(down_batch, 0, batch_count - 1)
        up_slot = jnp.clip(up_batch, 0, batch_count - 1)
        moved_down, moved_up = both_powers(send_down, send_up, down_live, up_live)
        new_down = lax.dynamic_index_in_dim(down_blocks, down_slot, 0, False) + moved_down
        new_up = lax.dynamic_index_in_dim(up_blocks, up_slot, 0, False) + moved_up
        kept_down = jnp.where(
            down_live, new_down, lax.dynamic_index_in_dim(out_down, down_slot, 0, False)
        )
        kept_up = jnp.where(up_live, new_up, lax.dynamic_index_in_dim(out_up, up_slot, 0, False))
        out_down = lax.dynamic_update_index_in_dim(out_down, kept_down, down_slot, 0)
        out_up = lax.dynamic_update_index_in_dim(out_up, kept_up, up_slot, 0)
        return (new_down.astype(jnp.bfloat16), new_up.astype(jnp.bfloat16), out_down, out_up)

    start_state = (
        jnp.zeros(trace_shape, jnp.bfloat16),
        jnp.zeros(trace_shape, jnp.bfloat16),
        jnp.zeros(down_blocks.shape, jnp.float32),
        jnp.zeros(up_blocks.shape, jnp.float32),
    )
    _, _, out_down, out_up = lax.fori_loop(0, layer_count + batch_count - 1, one_step, start_state)
    summed = out_down + out_up
    return summed.transpose(2, 0, 3, 1, 4).reshape(2, batch_count * COLS, block_rows * tile_width)[
        None
    ]


def solution(mesh):
    return jax.shard_map(
        shards,
        mesh=mesh,
        in_specs=(
            P("layer", "tile", None, None, None, None),
            P("layer", "tile", None, None, None, None),
            P("layer", None, None, "tile"),
            P("layer", None, None, "tile"),
            P("layer"),
        ),
        out_specs=P("layer", None, None, "tile"),
        check_vma=False,
    )
```

profile of v0, /device:TPU:31, one launch (start us, length us, event | category | flops | bytes accessed | tf_op | source)
XLA Modules:
  0.0 491.8 jit_solution(18095654112411297325)
XLA Ops:
  0.0 17.2 %copy_bitcast_fusion.2 = (bf16[4,3,2,512,512]{4,3,2,0,1:T(8,128)(2,1)}, bf16[4,3,2,512,512]{4,3,2,0,1:T(8,128)(2,1)}) fusion(bf16[1,4,3,2,512,512]{5,4,3,2,1,0:T(8,128)(2,1)} %param.16, bf16[1,4,3,2,512,512]{5,4,3,2,1,0:T(8,128)(2,1)} %param.15), kind=kLoop, calls=%fused_computation.126 | loop fusion | bytes 50331648 | tf_op jit(solution)/shard_map/squeeze | solution.py:48
  18.7 472.2 %while.21 = (s32[]{:T(128)}, bf16[4,2,8,512]{3,2,0,1:T(8,128)(2,1)S(1)}, bf16[4,2,8,512]{3,2,0,1:T(8,128)(2,1)S(1)}, f32[4,4,2,8,512]{4,3,1,2,0:T(8,128)S(1)}, f...) while((s32[]{:T(128)}, ...), condition=%wide.region_9.10_spmd.clone, body=%wide.region_0.9_spmd.clone.sunk | while | flops 807075840 | bytes 64619160 | solution.py:111
  28.0 3.3 collective-permute-done.3
  31.3 8.6 %conditional.13 = (f32[4,2,8,512]{3,2,0,1:T(8,128)S(1)}) conditional(s32[]{:T(128)} %convert_element_type.70, () %tuple.88, (bf16[4,3,2,512,512]{4,3,2,0,1:T(8,128)(2,1)}, bf16[6,2,2,8,512]{4,3,2,0,1:T(8,128)(2,1)S(1)}) %tuple.89), branch_computations={%region_3.3_spmd, %region_4.4_spmd} | conditional | flops 201523200 | bytes 14745608 | solution.py:74
  34.2 2.8 fusion.29
  37.0 2.8 fusion.42
  43.5 3.3 collective-permute-done.5
  55.0 3.3 collective-permute-done.3
  58.4 8.6 %conditional.13 = (f32[4,2,8,512]{3,2,0,1:T(8,128)S(1)}) conditional(s32[]{:T(128)} %convert_element_type.70, () %tuple.88, (bf16[4,3,2,512,512]{4,3,2,0,1:T(8,128)(2,1)}, bf16[6,2,2,8,512]{4,3,2,0,1:T(8,128)(2,1)S(1)}) %tuple.89), branch_computations={%region_3.3_spmd, %region_4.4_spmd} | conditional | flops 201523200 | bytes 14745608 | solution.py:74
  61.2 2.8 fusion.29
  64.1 2.8 fusion.42
  70.4 3.3 collective-permute-done.5
  74.0 5.0 %collective-permute-start = (bf16[4,2,8,512]{3,2,1,0:T(8,128)(2,1)S(1)}, bf16[4,2,8,512]{3,2,1,0:T(8,128)(2,1)S(1)}, u32[]{:S(2)}, u32[]{:S(2)}) collective-permute-start(bf16[4,2,8,512]{3,2,1,0:T(8,128)(2,1)S(1)} %copy_select_fusion.4), channel_id=1, source_target_pairs={{4,0},{8,4},{12,8},{16,12},{20,16},{24,20},{28,24},{5,1},{9,5},{13... | collective-permute-start | bytes 196616 | tf_op jit(solution)/shard_map/while/body/eval_jaxpr/ppermute | solution.py:12
  85.2 3.3 collective-permute-done.3
  88.5 8.6 %conditional.13 = (f32[4,2,8,512]{3,2,0,1:T(8,128)S(1)}) conditional(s32[]{:T(128)} %convert_element_type.70, () %tuple.88, (bf16[4,3,2,512,512]{4,3,2,0,1:T(8,128)(2,1)}, bf16[6,2,2,8,512]{4,3,2,0,1:T(8,128)(2,1)S(1)}) %tuple.89), branch_computations={%region_3.3_spmd, %region_4.4_spmd} | conditional | flops 201523200 | bytes 14745608 | solution.py:74
  91.3 2.8 fusion.29
  94.2 2.8 fusion.42
  100.5 3.3 collective-permute-done.5
  104.1 6.9 %collective-permute-start = (bf16[4,2,8,512]{3,2,1,0:T(8,128)(2,1)S(1)}, bf16[4,2,8,512]{3,2,1,0:T(8,128)(2,1)S(1)}, u32[]{:S(2)}, u32[]{:S(2)}) collective-permute-start(bf16[4,2,8,512]{3,2,1,0:T(8,128)(2,1)S(1)} %copy_select_fusion.4), channel_id=1, source_target_pairs={{4,0},{8,4},{12,8},{16,12},{20,16},{24,20},{28,24},{5,1},{9,5},{13... | collective-permute-start | bytes 196616 | tf_op jit(solution)/shard_map/while/body/eval_jaxpr/ppermute | solution.py:12
  112.5 6.7 %collective-permute-done.1 = bf16[4,2,8,512]{3,2,1,0:T(8,128)(2,1)S(1)} collective-permute-done((bf16[4,2,8,512]{3,2,1,0:T(8,128)(2,1)S(1)}, bf16[4,2,8,512]{3,2,1,0:T(8,128)(2,1)S(1)}, u32[]{:S(2)}, u32[]{:S(2)}) %collective-permute-start.1) | collective-permute-done | bytes 65568 | tf_op jit(solution)/shard_map/while/body/eval_jaxpr/ppermute | solution.py:12
  122.4 3.3 collective-permute-done.3
  125.8 8.6 %conditional.13 = (f32[4,2,8,512]{3,2,0,1:T(8,128)S(1)}) conditional(s32[]{:T(128)} %convert_element_type.70, () %tuple.88, (bf16[4,3,2,512,512]{4,3,2,0,1:T(8,128)(2,1)}, bf16[6,2,2,8,512]{4,3,2,0,1:T(8,128)(2,1)S(1)}) %tuple.89), branch_computations={%region_3.3_spmd, %region_4.4_spmd} | conditional | flops 201523200 | bytes 14745608 | solution.py:74
  128.6 2.8 fusion.29
  131.5 2.8 fusion.42
  137.7 3.3 collective-permute-done.5
  141.4 7.4 %collective-permute-start = (bf16[4,2,8,512]{3,2,1,0:T(8,128)(2,1)S(1)}, bf16[4,2,8,512]{3,2,1,0:T(8,128)(2,1)S(1)}, u32[]{:S(2)}, u32[]{:S(2)}) collective-permute-start(bf16[4,2,8,512]{3,2,1,0:T(8,128)(2,1)S(1)} %copy_select_fusion.4), channel_id=1, source_target_pairs={{4,0},{8,4},{12,8},{16,12},{20,16},{24,20},{28,24},{5,1},{9,5},{13... | collective-permute-start | bytes 196616 | tf_op jit(solution)/shard_map/while/body/eval_jaxpr/ppermute | solution.py:12
  150.2 7.0 %collective-permute-done.1 = bf16[4,2,8,512]{3,2,1,0:T(8,128)(2,1)S(1)} collective-permute-done((bf16[4,2,8,512]{3,2,1,0:T(8,128)(2,1)S(1)}, bf16[4,2,8,512]{3,2,1,0:T(8,128)(2,1)S(1)}, u32[]{:S(2)}, u32[]{:S(2)}) %collective-permute-start.1) | collective-permute-done | bytes 65568 | tf_op jit(solution)/shard_map/while/body/eval_jaxpr/ppermute | solution.py:12
  160.5 3.3 collective-permute-done.3
  167.2 3.3 collective-permute-done.5
  170.9 39.3 %collective-permute-start = (bf16[4,2,8,512]{3,2,1,0:T(8,128)(2,1)S(1)}, bf16[4,2,8,512]{3,2,1,0:T(8,128)(2,1)S(1)}, u32[]{:S(2)}, u32[]{:S(2)}) collective-permute-start(bf16[4,2,8,512]{3,2,1,0:T(8,128)(2,1)S(1)} %copy_select_fusion.4), channel_id=1, source_target_pairs={{4,0},{8,4},{12,8},{16,12},{20,16},{24,20},{28,24},{5,1},{9,5},{13... | collective-permute-start | bytes 196616 | tf_op jit(solution)/shard_map/while/body/eval_jaxpr/ppermute | solution.py:12
  211.6 6.7 %collective-permute-done.1 = bf16[4,2,8,512]{3,2,1,0:T(8,128)(2,1)S(1)} collective-permute-done((bf16[4,2,8,512]{3,2,1,0:T(8,128)(2,1)S(1)}, bf16[4,2,8,512]{3,2,1,0:T(8,128)(2,1)S(1)}, u32[]{:S(2)}, u32[]{:S(2)}) %collective-permute-start.1) | collective-permute-done | bytes 65568 | tf_op jit(solution)/shard_map/while/body/eval_jaxpr/ppermute | solution.py:12
  221.5 3.3 collective-permute-done.3
  228.3 3.3 collective-permute-done.5
  231.9 28.4 %collective-permute-start = (bf16[4,2,8,512]{3,2,1,0:T(8,128)(2,1)S(1)}, bf16[4,2,8,512]{3,2,1,0:T(8,128)(2,1)S(1)}, u32[]{:S(2)}, u32[]{:S(2)}) collective-permute-start(bf16[4,2,8,512]{3,2,1,0:T(8,128)(2,1)S(1)} %copy_select_fusion.4), channel_id=1, source_target_pairs={{4,0},{8,4},{12,8},{16,12},{20,16},{24,20},{28,24},{5,1},{9,5},{13... | collective-permute-start | bytes 196616 | tf_op jit(solution)/shard_map/while/body/eval_jaxpr/ppermute | solution.py:12
  261.8 32.4 %collective-permute-done.1 = bf16[4,2,8,512]{3,2,1,0:T(8,128)(2,1)S(1)} collective-permute-done((bf16[4,2,8,512]{3,2,1,0:T(8,128)(2,1)S(1)}, bf16[4,2,8,512]{3,2,1,0:T(8,128)(2,1)S(1)}, u32[]{:S(2)}, u32[]{:S(2)}) %collective-permute-start.1) | collective-permute-done | bytes 65568 | tf_op jit(solution)/shard_map/while/body/eval_jaxpr/ppermute | solution.py:12
  297.4 3.4 collective-permute-done.3
  304.2 3.3 collective-permute-done.5
  307.8 19.8 %collective-permute-start = (bf16[4,2,8,512]{3,2,1,0:T(8,128)(2,1)S(1)}, bf16[4,2,8,512]{3,2,1,0:T(8,128)(2,1)S(1)}, u32[]{:S(2)}, u32[]{:S(2)}) collective-permute-start(bf16[4,2,8,512]{3,2,1,0:T(8,128)(2,1)S(1)} %copy_select_fusion.4), channel_id=1, source_target_pairs={{4,0},{8,4},{12,8},{16,12},{20,16},{24,20},{28,24},{5,1},{9,5},{13... | collective-permute-start | bytes 196616 | tf_op jit(solution)/shard_map/while/body/eval_jaxpr/ppermute | solution.py:12
  329.1 6.7 %collective-permute-done.1 = bf16[4,2,8,512]{3,2,1,0:T(8,128)(2,1)S(1)} collective-permute-done((bf16[4,2,8,512]{3,2,1,0:T(8,128)(2,1)S(1)}, bf16[4,2,8,512]{3,2,1,0:T(8,128)(2,1)S(1)}, u32[]{:S(2)}, u32[]{:S(2)}) %collective-permute-start.1) | collective-permute-done | bytes 65568 | tf_op jit(solution)/shard_map/while/body/eval_jaxpr/ppermute | solution.py:12
  339.0 3.3 collective-permute-done.3
  342.4 8.6 %conditional.12 = (f32[4,2,8,512]{3,2,0,1:T(8,128)S(1)}) conditional(s32[]{:T(128)} %convert_element_type.69, () %tuple.86, (bf16[4,3,2,512,512]{4,3,2,0,1:T(8,128)(2,1)}, bf16[6,2,2,8,512]{4,3,2,0,1:T(8,128)(2,1)S(1)}) %tuple.87), branch_computations={%region_1.1_spmd, %region_2.2_spmd} | conditional | flops 201523200 | bytes 14745608 | solution.py:71
  345.3 2.8 fusion.2
  348.1 2.8 fusion.15
  354.3 3.3 collective-permute-done.5
  358.0 28.4 %collective-permute-start = (bf16[4,2,8,512]{3,2,1,0:T(8,128)(2,1)S(1)}, bf16[4,2,8,512]{3,2,1,0:T(8,128)(2,1)S(1)}, u32[]{:S(2)}, u32[]{:S(2)}) collective-permute-start(bf16[4,2,8,512]{3,2,1,0:T(8,128)(2,1)S(1)} %copy_select_fusion.4), channel_id=1, source_target_pairs={{4,0},{8,4},{12,8},{16,12},{20,16},{24,20},{28,24},{5,1},{9,5},{13... | collective-permute-start | bytes 196616 | tf_op jit(solution)/shard_map/while/body/eval_jaxpr/ppermute | solution.py:12
  387.8 6.7 %collective-permute-done.1 = bf16[4,2,8,512]{3,2,1,0:T(8,128)(2,1)S(1)} collective-permute-done((bf16[4,2,8,512]{3,2,1,0:T(8,128)(2,1)S(1)}, bf16[4,2,8,512]{3,2,1,0:T(8,128)(2,1)S(1)}, u32[]{:S(2)}, u32[]{:S(2)}) %collective-permute-start.1) | collective-permute-done | bytes 65568 | tf_op jit(solution)/shard_map/while/body/eval_jaxpr/ppermute | solution.py:12
  397.8 3.4 collective-permute-done.3
  401.2 8.6 %conditional.12 = (f32[4,2,8,512]{3,2,0,1:T(8,128)S(1)}) conditional(s32[]{:T(128)} %convert_element_type.69, () %tuple.86, (bf16[4,3,2,512,512]{4,3,2,0,1:T(8,128)(2,1)}, bf16[6,2,2,8,512]{4,3,2,0,1:T(8,128)(2,1)S(1)}) %tuple.87), branch_computations={%region_1.1_spmd, %region_2.2_spmd} | conditional | flops 201523200 | bytes 14745608 | solution.py:71
  404.1 2.8 fusion.2
  406.9 2.8 fusion.15
  413.1 3.3 collective-permute-done.5
  416.8 11.3 %collective-permute-start = (bf16[4,2,8,512]{3,2,1,0:T(8,128)(2,1)S(1)}, bf16[4,2,8,512]{3,2,1,0:T(8,128)(2,1)S(1)}, u32[]{:S(2)}, u32[]{:S(2)}) collective-permute-start(bf16[4,2,8,512]{3,2,1,0:T(8,128)(2,1)S(1)} %copy_select_fusion.4), channel_id=1, source_target_pairs={{4,0},{8,4},{12,8},{16,12},{20,16},{24,20},{28,24},{5,1},{9,5},{13... | collective-permute-start | bytes 196616 | tf_op jit(solution)/shard_map/while/body/eval_jaxpr/ppermute | solution.py:12
  429.4 6.7 %collective-permute-done.1 = bf16[4,2,8,512]{3,2,1,0:T(8,128)(2,1)S(1)} collective-permute-done((bf16[4,2,8,512]{3,2,1,0:T(8,128)(2,1)S(1)}, bf16[4,2,8,512]{3,2,1,0:T(8,128)(2,1)S(1)}, u32[]{:S(2)}, u32[]{:S(2)}) %collective-permute-start.1) | collective-permute-done | bytes 65568 | tf_op jit(solution)/shard_map/while/body/eval_jaxpr/ppermute | solution.py:12
  439.4 3.3 collective-permute-done.3
  442.8 8.6 %conditional.12 = (f32[4,2,8,512]{3,2,0,1:T(8,128)S(1)}) conditional(s32[]{:T(128)} %convert_element_type.69, () %tuple.86, (bf16[4,3,2,512,512]{4,3,2,0,1:T(8,128)(2,1)}, bf16[6,2,2,8,512]{4,3,2,0,1:T(8,128)(2,1)S(1)}) %tuple.87), branch_computations={%region_1.1_spmd, %region_2.2_spmd} | conditional | flops 201523200 | bytes 14745608 | solution.py:71
  445.6 2.8 fusion.2
  448.5 2.8 fusion.15
  454.7 3.3 collective-permute-done.5
  458.4 7.4 %collective-permute-start = (bf16[4,2,8,512]{3,2,1,0:T(8,128)(2,1)S(1)}, bf16[4,2,8,512]{3,2,1,0:T(8,128)(2,1)S(1)}, u32[]{:S(2)}, u32[]{:S(2)}) collective-permute-start(bf16[4,2,8,512]{3,2,1,0:T(8,128)(2,1)S(1)} %copy_select_fusion.4), channel_id=1, source_target_pairs={{4,0},{8,4},{12,8},{16,12},{20,16},{24,20},{28,24},{5,1},{9,5},{13... | collective-permute-start | bytes 196616 | tf_op jit(solution)/shard_map/while/body/eval_jaxpr/ppermute | solution.py:12
  472.0 3.3 collective-permute-done.3
  475.4 8.6 %conditional.12 = (f32[4,2,8,512]{3,2,0,1:T(8,128)S(1)}) conditional(s32[]{:T(128)} %convert_element_type.69, () %tuple.86, (bf16[4,3,2,512,512]{4,3,2,0,1:T(8,128)(2,1)}, bf16[6,2,2,8,512]{4,3,2,0,1:T(8,128)(2,1)S(1)}) %tuple.87), branch_computations={%region_1.1_spmd, %region_2.2_spmd} | conditional | flops 201523200 | bytes 14745608 | solution.py:71
  478.2 2.8 fusion.2
  481.1 2.8 fusion.15
  487.3 3.3 collective-permute-done.5
  (342 shorter events, 125.9 us)
Async XLA Ops:
  18.8 4.0 collective-permute-start
  21.4 3.1 collective-permute-start.1
  24.5 3.4 collective-permute-start.2
  26.6 4.7 collective-permute-start.3
  40.0 3.4 collective-permute-start.4
  42.1 4.7 collective-permute-start.5
  48.4 3.1 collective-permute-start.1
  51.6 3.4 collective-permute-start.2
  53.7 4.7 collective-permute-start.3
  67.1 3.3 collective-permute-start.4
  69.0 4.7 collective-permute-start.5
  74.0 6.3 %collective-permute-start = (bf16[4,2,8,512]{3,2,1,0:T(8,128)(2,1)S(1)}, bf16[4,2,8,512]{3,2,1,0:T(8,128)(2,1)S(1)}, u32[]{:S(2)}, u32[]{:S(2)}) collective-permute-start(bf16[4,2,8,512]{3,2,1,0:T(8,128)(2,1)S(1)} %copy_select_fusion.4), channel_id=1, source_target_pairs={{4,0},{8,4},{12,8},{16,12},{20,16},{24,20},{28,24},{5,1},{9,5},{13... | collective-permute-start | bytes 196616 | tf_op jit(solution)/shard_map/while/body/eval_jaxpr/ppermute | solution.py:12
  79.0 3.1 collective-permute-start.1
  82.1 3.0 collective-permute-start.2
  83.8 4.7 collective-permute-start.3
  97.2 3.3 collective-permute-start.4
  99.1 4.7 collective-permute-start.5
  104.1 8.3 %collective-permute-start = (bf16[4,2,8,512]{3,2,1,0:T(8,128)(2,1)S(1)}, bf16[4,2,8,512]{3,2,1,0:T(8,128)(2,1)S(1)}, u32[]{:S(2)}, u32[]{:S(2)}) collective-permute-start(bf16[4,2,8,512]{3,2,1,0:T(8,128)(2,1)S(1)} %copy_select_fusion.4), channel_id=1, source_target_pairs={{4,0},{8,4},{12,8},{16,12},{20,16},{24,20},{28,24},{5,1},{9,5},{13... | collective-permute-start | bytes 196616 | tf_op jit(solution)/shard_map/while/body/eval_jaxpr/ppermute | solution.py:12
  111.1 8.0 %collective-permute-start.1 = (bf16[4,2,8,512]{3,2,1,0:T(8,128)(2,1)S(1)}, bf16[4,2,8,512]{3,2,1,0:T(8,128)(2,1)S(1)}, u32[]{:S(2)}, u32[]{:S(2)}) collective-permute-start(bf16[4,2,8,512]{3,2,1,0:T(8,128)(2,1)S(1)} %copy_select_fusion.5), channel_id=1, source_target_pairs={{0,4},{4,8},{8,12},{12,16},{16,20},{20,24},{24,28},{1,5},{5,9},{9,... | collective-permute-start | bytes 196616 | tf_op jit(solution)/shard_map/while/body/eval_jaxpr/ppermute | solution.py:12
  119.1 3.3 collective-permute-start.2
  121.1 4.7 collective-permute-start.3
  134.5 3.3 collective-permute-start.4
  136.4 4.7 collective-permute-start.5
  141.4 8.8 %collective-permute-start = (bf16[4,2,8,512]{3,2,1,0:T(8,128)(2,1)S(1)}, bf16[4,2,8,512]{3,2,1,0:T(8,128)(2,1)S(1)}, u32[]{:S(2)}, u32[]{:S(2)}) collective-permute-start(bf16[4,2,8,512]{3,2,1,0:T(8,128)(2,1)S(1)} %copy_select_fusion.4), channel_id=1, source_target_pairs={{4,0},{8,4},{12,8},{16,12},{20,16},{24,20},{28,24},{5,1},{9,5},{13... | collective-permute-start | bytes 196616 | tf_op jit(solution)/shard_map/while/body/eval_jaxpr/ppermute | solution.py:12
  148.9 8.3 %collective-permute-start.1 = (bf16[4,2,8,512]{3,2,1,0:T(8,128)(2,1)S(1)}, bf16[4,2,8,512]{3,2,1,0:T(8,128)(2,1)S(1)}, u32[]{:S(2)}, u32[]{:S(2)}) collective-permute-start(bf16[4,2,8,512]{3,2,1,0:T(8,128)(2,1)S(1)} %copy_select_fusion.5), channel_id=1, source_target_pairs={{0,4},{4,8},{8,12},{12,16},{16,20},{20,24},{24,28},{1,5},{5,9},{9,... | collective-permute-start | bytes 196616 | tf_op jit(solution)/shard_map/while/body/eval_jaxpr/ppermute | solution.py:12
  157.2 3.3 collective-permute-start.2
  159.1 4.7 collective-permute-start.3
  164.0 3.3 collective-permute-start.4
  165.9 4.7 collective-permute-start.5
  170.9 40.7 %collective-permute-start = (bf16[4,2,8,512]{3,2,1,0:T(8,128)(2,1)S(1)}, bf16[4,2,8,512]{3,2,1,0:T(8,128)(2,1)S(1)}, u32[]{:S(2)}, u32[]{:S(2)}) collective-permute-start(bf16[4,2,8,512]{3,2,1,0:T(8,128)(2,1)S(1)} %copy_select_fusion.4), channel_id=1, source_target_pairs={{4,0},{8,4},{12,8},{16,12},{20,16},{24,20},{28,24},{5,1},{9,5},{13... | collective-permute-start | bytes 196616 | tf_op jit(solution)/shard_map/while/body/eval_jaxpr/ppermute | solution.py:12
  210.2 8.0 %collective-permute-start.1 = (bf16[4,2,8,512]{3,2,1,0:T(8,128)(2,1)S(1)}, bf16[4,2,8,512]{3,2,1,0:T(8,128)(2,1)S(1)}, u32[]{:S(2)}, u32[]{:S(2)}) collective-permute-start(bf16[4,2,8,512]{3,2,1,0:T(8,128)(2,1)S(1)} %copy_select_fusion.5), channel_id=1, source_target_pairs={{0,4},{4,8},{8,12},{12,16},{16,20},{20,24},{24,28},{1,5},{5,9},{9,... | collective-permute-start | bytes 196616 | tf_op jit(solution)/shard_map/while/body/eval_jaxpr/ppermute | solution.py:12
  218.2 3.3 collective-permute-start.2
  220.2 4.7 collective-permute-start.3
  225.0 3.3 collective-permute-start.4
  226.9 4.7 collective-permute-start.5
  231.9 29.8 %collective-permute-start = (bf16[4,2,8,512]{3,2,1,0:T(8,128)(2,1)S(1)}, bf16[4,2,8,512]{3,2,1,0:T(8,128)(2,1)S(1)}, u32[]{:S(2)}, u32[]{:S(2)}) collective-permute-start(bf16[4,2,8,512]{3,2,1,0:T(8,128)(2,1)S(1)} %copy_select_fusion.4), channel_id=1, source_target_pairs={{4,0},{8,4},{12,8},{16,12},{20,16},{24,20},{28,24},{5,1},{9,5},{13... | collective-permute-start | bytes 196616 | tf_op jit(solution)/shard_map/while/body/eval_jaxpr/ppermute | solution.py:12
  260.4 33.8 %collective-permute-start.1 = (bf16[4,2,8,512]{3,2,1,0:T(8,128)(2,1)S(1)}, bf16[4,2,8,512]{3,2,1,0:T(8,128)(2,1)S(1)}, u32[]{:S(2)}, u32[]{:S(2)}) collective-permute-start(bf16[4,2,8,512]{3,2,1,0:T(8,128)(2,1)S(1)} %copy_select_fusion.5), channel_id=1, source_target_pairs={{0,4},{4,8},{8,12},{12,16},{16,20},{20,24},{24,28},{1,5},{5,9},{9,... | collective-permute-start | bytes 196616 | tf_op jit(solution)/shard_map/while/body/eval_jaxpr/ppermute | solution.py:12
  294.1 3.3 collective-permute-start.2
  296.1 4.7 collective-permute-start.3
  301.0 3.2 collective-permute-start.4
  302.8 4.7 collective-permute-start.5
  307.8 21.2 %collective-permute-start = (bf16[4,2,8,512]{3,2,1,0:T(8,128)(2,1)S(1)}, bf16[4,2,8,512]{3,2,1,0:T(8,128)(2,1)S(1)}, u32[]{:S(2)}, u32[]{:S(2)}) collective-permute-start(bf16[4,2,8,512]{3,2,1,0:T(8,128)(2,1)S(1)} %copy_select_fusion.4), channel_id=1, source_target_pairs={{4,0},{8,4},{12,8},{16,12},{20,16},{24,20},{28,24},{5,1},{9,5},{13... | collective-permute-start | bytes 196616 | tf_op jit(solution)/shard_map/while/body/eval_jaxpr/ppermute | solution.py:12
  327.7 8.0 %collective-permute-start.1 = (bf16[4,2,8,512]{3,2,1,0:T(8,128)(2,1)S(1)}, bf16[4,2,8,512]{3,2,1,0:T(8,128)(2,1)S(1)}, u32[]{:S(2)}, u32[]{:S(2)}) collective-permute-start(bf16[4,2,8,512]{3,2,1,0:T(8,128)(2,1)S(1)} %copy_select_fusion.5), channel_id=1, source_target_pairs={{0,4},{4,8},{8,12},{12,16},{16,20},{20,24},{24,28},{1,5},{5,9},{9,... | collective-permute-start | bytes 196616 | tf_op jit(solution)/shard_map/while/body/eval_jaxpr/ppermute | solution.py:12
  335.7 3.3 collective-permute-start.2
  337.7 4.7 collective-permute-start.3
  351.1 3.3 collective-permute-start.4
  353.0 4.7 collective-permute-start.5
  358.0 29.8 %collective-permute-start = (bf16[4,2,8,512]{3,2,1,0:T(8,128)(2,1)S(1)}, bf16[4,2,8,512]{3,2,1,0:T(8,128)(2,1)S(1)}, u32[]{:S(2)}, u32[]{:S(2)}) collective-permute-start(bf16[4,2,8,512]{3,2,1,0:T(8,128)(2,1)S(1)} %copy_select_fusion.4), channel_id=1, source_target_pairs={{4,0},{8,4},{12,8},{16,12},{20,16},{24,20},{28,24},{5,1},{9,5},{13... | collective-permute-start | bytes 196616 | tf_op jit(solution)/shard_map/while/body/eval_jaxpr/ppermute | solution.py:12
  386.4 8.0 %collective-permute-start.1 = (bf16[4,2,8,512]{3,2,1,0:T(8,128)(2,1)S(1)}, bf16[4,2,8,512]{3,2,1,0:T(8,128)(2,1)S(1)}, u32[]{:S(2)}, u32[]{:S(2)}) collective-permute-start(bf16[4,2,8,512]{3,2,1,0:T(8,128)(2,1)S(1)} %copy_select_fusion.5), channel_id=1, source_target_pairs={{0,4},{4,8},{8,12},{12,16},{16,20},{20,24},{24,28},{1,5},{5,9},{9,... | collective-permute-start | bytes 196616 | tf_op jit(solution)/shard_map/while/body/eval_jaxpr/ppermute | solution.py:12
  394.5 3.3 collective-permute-start.2
  396.4 4.7 collective-permute-start.3
  409.9 3.2 collective-permute-start.4
  411.8 4.7 collective-permute-start.5
  416.8 12.7 %collective-permute-start = (bf16[4,2,8,512]{3,2,1,0:T(8,128)(2,1)S(1)}, bf16[4,2,8,512]{3,2,1,0:T(8,128)(2,1)S(1)}, u32[]{:S(2)}, u32[]{:S(2)}) collective-permute-start(bf16[4,2,8,512]{3,2,1,0:T(8,128)(2,1)S(1)} %copy_select_fusion.4), channel_id=1, source_target_pairs={{4,0},{8,4},{12,8},{16,12},{20,16},{24,20},{28,24},{5,1},{9,5},{13... | collective-permute-start | bytes 196616 | tf_op jit(solution)/shard_map/while/body/eval_jaxpr/ppermute | solution.py:12
  428.0 8.0 %collective-permute-start.1 = (bf16[4,2,8,512]{3,2,1,0:T(8,128)(2,1)S(1)}, bf16[4,2,8,512]{3,2,1,0:T(8,128)(2,1)S(1)}, u32[]{:S(2)}, u32[]{:S(2)}) collective-permute-start(bf16[4,2,8,512]{3,2,1,0:T(8,128)(2,1)S(1)} %copy_select_fusion.5), channel_id=1, source_target_pairs={{0,4},{4,8},{8,12},{12,16},{16,20},{20,24},{24,28},{1,5},{5,9},{9,... | collective-permute-start | bytes 196616 | tf_op jit(solution)/shard_map/while/body/eval_jaxpr/ppermute | solution.py:12
  436.1 3.3 collective-permute-start.2
  438.0 4.7 collective-permute-start.3
  451.4 3.3 collective-permute-start.4
  453.3 4.7 collective-permute-start.5
  458.4 8.8 %collective-permute-start = (bf16[4,2,8,512]{3,2,1,0:T(8,128)(2,1)S(1)}, bf16[4,2,8,512]{3,2,1,0:T(8,128)(2,1)S(1)}, u32[]{:S(2)}, u32[]{:S(2)}) collective-permute-start(bf16[4,2,8,512]{3,2,1,0:T(8,128)(2,1)S(1)} %copy_select_fusion.4), channel_id=1, source_target_pairs={{4,0},{8,4},{12,8},{16,12},{20,16},{24,20},{28,24},{5,1},{9,5},{13... | collective-permute-start | bytes 196616 | tf_op jit(solution)/shard_map/while/body/eval_jaxpr/ppermute | solution.py:12
  465.8 3.1 collective-permute-start.1
  470.6 4.7 collective-permute-start.3
  484.0 3.3 collective-permute-start.4
  485.9 4.7 collective-permute-start.5
  (4 other events, 40.5 us)
where the time goes:
time: 484 us; the launch traced here: 492 us
  starting transfers between devices  242 us (50%)
  waiting for transfers between devices  153 us (32%)
  matrix products  68.2 us (14%)
  local copies, waits for them, and re-layouts  20 us (4%)
    ppermute x22, starting transfers between devices, passed_along(): lax.ppermute(value, axis, [(source, source + steps) for source in range(l...  172 us
    ppermute x22, waiting for transfers between devices, passed_along(): lax.ppermute(value, axis, [(source, source + steps) for source in range(l...  79.7 us
    ppermute x22, waiting for transfers between devices, extended_2(): lax.ppermute(lax.slice_in_dim(block, block.shape[dim] - width, None, axis...  72.9 us
    dot_general x24, matrix products, combine(): jnp.einsum('bpct,bqtu->bpqcu', inputs[offset:offset + block_rows], layer_...  68.2 us
    ppermute x22, starting transfers between devices, extended_2(): lax.ppermute(lax.slice_in_dim(block, 0, width, axis=dim), axis, backward)  42 us
    ppermute x22, starting transfers between devices, extended_2(): lax.ppermute(lax.slice_in_dim(block, block.shape[dim] - width, None, axis...  28.4 us
    squeeze x1, local copies, waits for them, and re-layouts, shards(): own_up = up_tiles[0]  17.2 us
  transfers between devices with their start and end apart: 66, of which 33 were waited for; matrix products, arithmetic and copies ran while one was open for 0% of the time, Pallas kernels for 0%

commit v1 on v0

v1 whole, which is shorter than its diff:
```python
import functools

import jax
import jax.numpy as jnp
from jax import lax
from jax.experimental import pallas as pl
from jax.experimental.pallas import tpu as pltpu
from jax.sharding import PartitionSpec as P

MESH = pl.DeviceIdType.MESH


def sweep_kernel(
    layers, tiles, rows, width, cols,
    down_tiles, up_tiles, down_source, up_source, thick_ref, out_ref,
    weights, source, inbox, wide, accum, first, outbox,
    tile_sem, source_sem, recv_sem, next_sem, rim_sem, mid_sem,
):
    layer = lax.axis_index("layer")
    tile = lax.axis_index("tile")
    height = 2 * cols
    depth = 2 * width
    slots = rows + 2
    has_low, has_high = tile > 0, tile < tiles - 1
    own_first = jnp.where(2 * layer < layers, 0, 1)

    groups = [g for g in (list(range(2, rows)), sorted({1, rows}), [0, rows + 1]) if g]

    def tile_copy(ref, direction, b, k):
        return pltpu.make_async_copy(
            ref.at[b, pl.ds(k * depth, depth)],
            weights.at[direction, b, pl.ds(k * depth, depth)],
            tile_sem.at[direction, b, k],
        )

    def source_copy(ref, direction, b):
        return pltpu.make_async_copy(
            ref.at[:, pl.ds(b * width, width)], source.at[direction, b], source_sem.at[direction, b]
        )

    tile_order = [(b, j - b) for g in groups for j in g for b in range(rows) if 0 <= j - b <= 2]

    def start_loads(ref, direction):
        for b, k in tile_order:
            tile_copy(ref, direction, b, k).start()

    for direction, ref in enumerate((down_source, up_source)):
        for b in range(rows):
            source_copy(ref, direction, b).start()

    @pl.when(own_first == 0)
    def _():
        start_loads(down_tiles, 0)
        start_loads(up_tiles, 1)

    @pl.when(own_first == 1)
    def _():
        start_loads(up_tiles, 1)
        start_loads(down_tiles, 0)

    barrier = pltpu.get_barrier_semaphore()
    met = 0
    for dl in (-1, 0, 1):
        for dt in (-1, 0, 1):
            if dl == 0 and dt == 0:
                continue
            there = (layer + dl >= 0) & (layer + dl < layers) & (tile + dt >= 0) & (tile + dt < tiles)

            @pl.when(there)
            def _(dl=dl, dt=dt):
                pl.semaphore_signal(
                    barrier, inc=1, device_id={"layer": layer + dl, "tile": tile + dt}, device_id_type=MESH
                )

            met = met + jnp.where(there, 1, 0)

    out_ref[...] = jnp.zeros_like(out_ref)
    no_trace = jnp.zeros((height, width), jnp.bfloat16)

    @pl.when(jnp.logical_not(has_low))
    def _():
        for direction in range(2):
            for phase in range(2):
                inbox[direction, phase, 0] = no_trace

    @pl.when(jnp.logical_not(has_high))
    def _():
        for direction in range(2):
            for phase in range(2):
                inbox[direction, phase, rows + 1] = no_trace

    pl.semaphore_wait(barrier, met)
    is_thick = jnp.full((height, width), thick_ref[0], jnp.int32) == 2

    def remote(src, direction, phase, slot, send_sem, to_layer, to_tile):
        return pltpu.make_async_remote_copy(
            src_ref=src,
            dst_ref=inbox.at[direction, phase, slot],
            send_sem=send_sem,
            recv_sem=recv_sem.at[direction, phase, slot],
            device_id={"layer": to_layer, "tile": to_tile},
            device_id_type=MESH,
        )

    def onward(direction, b):
        to_layer = layer + 1 - 2 * direction
        box = outbox.at[direction, b]
        copies = []
        if b == 0:
            copies.append((has_low, remote(
                box, direction, 0, rows + 1, rim_sem.at[direction, 0], to_layer, tile - 1)))
        if b == rows - 1:
            copies.append((has_high, remote(
                box, direction, 0, 0, rim_sem.at[direction, 1], to_layer, tile + 1)))
        copies.append((None, remote(
            box, direction, 0, b + 1, next_sem.at[direction, b], to_layer, tile)))
        return copies

    def sideways(direction, b):
        box = inbox.at[direction, 1, b + 1]
        copies = []
        if b == 0:
            copies.append((has_low, remote(
                box, direction, 1, rows + 1, mid_sem.at[direction, 0], layer, tile - 1)))
        if b == rows - 1:
            copies.append((has_high, remote(
                box, direction, 1, 0, mid_sem.at[direction, 1], layer, tile + 1)))
        return copies

    def each(copies, what):
        for condition, copy in copies:
            if condition is None:
                what(copy)
            else:
                pl.when(condition)(functools.partial(what, copy))

    def start(copy):
        copy.start()

    def sent(copy):
        copy.wait_send()

    def arrived(direction, phase, slot):
        def wait():
            remote(
                inbox.at[direction, phase, slot], direction, phase, slot,
                mid_sem.at[direction, 0], layer, tile,
            ).wait_recv()

        if slot == 0:
            pl.when(has_low)(wait)
        elif slot == rows + 1:
            pl.when(has_high)(wait)
        else:
            pl.when(phase == 0)(wait)

    def finish(direction, b, moved, has_next):
        columns = pl.ds(b * width, width)
        source_copy(down_source, direction, b).wait()
        value = source[direction, b]
        if moved is not None:
            value = value + moved
        out_ref[:, columns] += value

        @pl.when(has_next)
        def _():
            outbox[direction, b] = value.astype(jnp.bfloat16)
            each(onward(direction, b), start)

    def one_phase(phase, direction, has_next):
        touched = set()
        done = 0
        for group in groups:
            for j in group:
                arrived(direction, phase, j)
                x = inbox[direction, phase, j]
                wide[:, pl.ds(j * depth, width)] = x
                wide[:, pl.ds(j * depth + width, width)] = jnp.concatenate([-x[cols:], x[:cols]], axis=0)
            outs = [b for b in range(rows) if any(0 <= j - b <= 2 for j in group)]
            ready = []
            for b in outs:
                taps = [j - b for j in group if 0 <= j - b <= 2]

                @pl.when(phase == 0)
                def _(b=b, taps=taps):
                    for k in taps:
                        tile_copy(down_tiles, direction, b, k).wait()

                runs = []
                for k in taps:
                    if runs and runs[-1][1] == k:
                        runs[-1][1] = k + 1
                    else:
                        runs.append([k, k + 1])
                total = None
                for low, high in runs:
                    part = jnp.dot(
                        wide[:, pl.ds((b + low) * depth, (high - low) * depth)],
                        weights[direction, b, pl.ds(low * depth, (high - low) * depth)],
                        preferred_element_type=jnp.float32,
                    )
                    total = part if total is None else total + part
                accum[b] = accum[b] + total if b in touched else total
                touched.add(b)
                done |= sum(1 << (3 * b + k) for k in taps)
                if (done >> (3 * b)) & 7 == 7:
                    ready.append(b)

                    @pl.when(phase == 0)
                    def _(b=b):
                        first[b] = accum[b]
                        inbox[direction, 1, b + 1] = accum[b].astype(jnp.bfloat16)
                        each(sideways(direction, b), start)

                    @pl.when(phase == 1)
                    def _(b=b):
                        finish(direction, b, jnp.where(is_thick, accum[b], first[b]), has_next)

    def one_direction(step, carry):
        direction = (own_first + step) % 2
        begins = jnp.where(direction == 0, layer == 0, layer == layers - 1)
        has_next = jnp.where(direction == 0, layer < layers - 1, layer > 0)

        @pl.when(begins)
        def _():
            for b in sorted(range(rows), key=lambda b: 0 < b < rows - 1):
                finish(direction, b, None, has_next)
            for b, k in tile_order:
                tile_copy(down_tiles, direction, b, k).wait()

        @pl.when(jnp.logical_not(begins))
        def _():
            def body(phase, inner):
                one_phase(phase, direction, has_next)
                return inner

            lax.fori_loop(0, 2, body, 0)
            for b in range(rows):
                each(sideways(direction, b), sent)

        return carry

    lax.fori_loop(0, 2, one_direction, 0)
    for direction in range(2):
        has_next = layer < layers - 1 if direction == 0 else layer > 0

        @pl.when(has_next)
        def _(direction=direction):
            for b in range(rows):
                each(onward(direction, b), sent)


def shards(layers, tiles, down_tiles, up_tiles, down_source, up_source, thickness):
    _, rows, taps, parts, width, _ = down_tiles.shape
    cols = down_source.shape[2]
    height, depth = parts * cols, parts * width
    points = rows * width
    flat_tiles = (rows, taps * depth, width)
    flat = (height, points)
    anywhere = pl.BlockSpec(memory_space=pl.ANY)
    field = pl.pallas_call(
        functools.partial(sweep_kernel, layers, tiles, rows, width, cols),
        out_shape=jax.ShapeDtypeStruct(flat, jnp.float32),
        in_specs=[anywhere] * 4 + [pl.BlockSpec(memory_space=pltpu.SMEM)],
        out_specs=pl.BlockSpec(memory_space=pltpu.VMEM),
        scratch_shapes=[
            pltpu.VMEM((2,) + flat_tiles, jnp.bfloat16),
            pltpu.VMEM((2, rows, height, width), jnp.float32),
            pltpu.VMEM((2, 2, rows + 2, height, width), jnp.bfloat16),
            pltpu.VMEM((height, (rows + 2) * depth), jnp.bfloat16),
            pltpu.VMEM((rows, height, width), jnp.float32),
            pltpu.VMEM((rows, height, width), jnp.float32),
            pltpu.VMEM((2, rows, height, width), jnp.bfloat16),
            pltpu.SemaphoreType.DMA((2, rows, taps)),
            pltpu.SemaphoreType.DMA((2, rows)),
            pltpu.SemaphoreType.DMA((2, 2, rows + 2)),
            pltpu.SemaphoreType.DMA((2, rows)),
            pltpu.SemaphoreType.DMA((2, 2)),
            pltpu.SemaphoreType.DMA((2, 2)),
        ],
        compiler_params=pltpu.CompilerParams(
            collective_id=0, has_side_effects=True, vmem_limit_bytes=48 * 1024 * 1024
        ),
        cost_estimate=pl.CostEstimate(
            flops=8 * rows * taps * height * depth * width,
            bytes_accessed=4 * rows * taps * depth * width,
            transcendentals=0,
        ),
    )(
        down_tiles.reshape(flat_tiles),
        up_tiles.reshape(flat_tiles),
        down_source.reshape(flat),
        up_source.reshape(flat),
        thickness,
    )
    return field.reshape(down_source.shape)


def solution(mesh):
    return jax.shard_map(
        functools.partial(shards, mesh.shape["layer"], mesh.shape["tile"]),
        mesh=mesh,
        in_specs=(
            P("layer", "tile", None, None, None, None),
            P("layer", "tile", None, None, None, None),
            P("layer", None, None, "tile"),
            P("layer", None, None, "tile"),
            P("layer"),
        ),
        out_specs=P("layer", None, None, "tile"),
        check_vma=False,
    )
```

time: 484 us -> 66.5 us (0.14)
  the two profiles are of different devices: /device:TPU:31 before, /device:TPU:0 now
where the time goes in v1:
time: 66.5 us; the launch traced here: 66.3 us
  Pallas kernels  62.8 us (94%)
  local copies, waits for them, and re-layouts  2.87 us (4%)
  between operations  0.67 us (1%)
    pallas_call x1, Pallas kernels, shards(): pl.pallas_call(functools.partial(sweep_kernel, layers, tiles, rows, width...  62.8 us
    unnamed x5, local copies, waits for them, and re-layouts  2.87 us

profile of v1, /device:TPU:0, one launch (start us, length us, event | category | flops | bytes accessed | tf_op | source)
XLA Modules:
  0.0 66.3 jit_solution(12463511531142543221)
XLA Ops:
  0.7 0.0 copy-start
  0.7 1.0 %copy-done = f32[1,2,32,2048]{3,2,1,0:T(8,128)S(1)} copy-done((f32[1,2,32,2048]{3,2,1,0:T(8,128)S(1)}, f32[1,2,32,2048]{3,2,1,0:T(8,128)}, u32[]{:S(2)}) %copy-start) | copy-done | bytes 524312
  1.7 0.0 copy-start.1
  1.7 1.0 %copy-done.1 = f32[1,2,32,2048]{3,2,1,0:T(8,128)S(1)} copy-done((f32[1,2,32,2048]{3,2,1,0:T(8,128)S(1)}, f32[1,2,32,2048]{3,2,1,0:T(8,128)}, u32[]{:S(2)}) %copy-start.1) | copy-done | bytes 524312
  2.7 62.8 %shard_map.55 = f32[64,2048]{1,0:T(8,128)S(1)} custom-call(bf16[4,3072,512]{2,1,0:T(8,128)(2,1)} %bitcast.8, bf16[4,3072,512]{2,1,0:T(8,128)(2,1)} %bitcast.9, f32[64,2048]{1,0:T(8,128)S(1)} %bitcast.6, f32[64,2048]{1,0:T(8,128)S(1)} %bitcast.7, s32[1]{0:T(128)S(6)} %copy.7.thick_ref), custom_call_target="tpu_custom_call" | custom-call | flops 3221225472 | bytes 25165824 | tf_op jit(solution)/shard_map/pallas_call | solution.py:261
  65.5 0.8 %copy.8 = f32[1,2,32,2048]{3,2,1,0:T(8,128)} copy(f32[1,2,32,2048]{3,2,1,0:T(8,128)S(1)} %bitcast.5) | data formatting | bytes 1048576
Async XLA Ops:
  0.7 1.0 %copy-start = (f32[1,2,32,2048]{3,2,1,0:T(8,128)S(1)}, f32[1,2,32,2048]{3,2,1,0:T(8,128)}, u32[]{:S(2)}) copy-start(f32[1,2,32,2048]{3,2,1,0:T(8,128)} %param.7) | copy-start | bytes 1572868
  1.7 1.0 %copy-start.1 = (f32[1,2,32,2048]{3,2,1,0:T(8,128)S(1)}, f32[1,2,32,2048]{3,2,1,0:T(8,128)}, u32[]{:S(2)}) copy-start(f32[1,2,32,2048]{3,2,1,0:T(8,128)} %param.8) | copy-start | bytes 1572868

commit v2 on v1

--- a/solution.py
+++ b/solution.py
@@ -13,7 +13,7 @@
 def sweep_kernel(
     layers, tiles, rows, width, cols,
     down_tiles, up_tiles, down_source, up_source, thick_ref, out_ref,
-    weights, source, inbox, wide, accum, first, outbox,
+    weights, source, inbox, wide, accum, outbox,
     tile_sem, source_sem, recv_sem, next_sem, rim_sem, mid_sem,
 ):
     layer = lax.axis_index("layer")
@@ -169,30 +169,31 @@
 
     def one_phase(phase, direction, has_next):
         touched = set()
-        done = 0
-        for group in groups:
+        edges = [b for b in range(rows) if b in (0, rows - 1)]
+        for position, group in enumerate(groups):
+            taps_of = {b: [j - b for j in group if 0 <= j - b <= 2] for b in range(rows)}
+            taps_of = {b: taps for b, taps in taps_of.items() if taps}
+
+            @pl.when(phase == 0)
+            def _(taps_of=taps_of):
+                for b, taps in taps_of.items():
+                    for k in taps:
+                        tile_copy(down_tiles, direction, b, k).wait()
+
             for j in group:
                 arrived(direction, phase, j)
+            for j in group:
                 x = inbox[direction, phase, j]
                 wide[:, pl.ds(j * depth, width)] = x
                 wide[:, pl.ds(j * depth + width, width)] = jnp.concatenate([-x[cols:], x[:cols]], axis=0)
-            outs = [b for b in range(rows) if any(0 <= j - b <= 2 for j in group)]
-            ready = []
-            for b in outs:
-                taps = [j - b for j in group if 0 <= j - b <= 2]
-
-                @pl.when(phase == 0)
-                def _(b=b, taps=taps):
-                    for k in taps:
-                        tile_copy(down_tiles, direction, b, k).wait()
-
+            for b, taps in taps_of.items():
                 runs = []
                 for k in taps:
                     if runs and runs[-1][1] == k:
                         runs[-1][1] = k + 1
                     else:
                         runs.append([k, k + 1])
-                total = None
+                total = accum[phase, b] if b in touched else None
                 for low, high in runs:
                     part = jnp.dot(
                         wide[:, pl.ds((b + low) * depth, (high - low) * depth)],
@@ -200,21 +201,25 @@
                         preferred_element_type=jnp.float32,
                     )
                     total = part if total is None else total + part
-                accum[b] = accum[b] + total if b in touched else total
+                accum[phase, b] = total
                 touched.add(b)
-                done |= sum(1 << (3 * b + k) for k in taps)
-                if (done >> (3 * b)) & 7 == 7:
-                    ready.append(b)
-
-                    @pl.when(phase == 0)
-                    def _(b=b):
-                        first[b] = accum[b]
-                        inbox[direction, 1, b + 1] = accum[b].astype(jnp.bfloat16)
+            last = position == len(groups) - 1
+            if last:
+                inner = [b for b in range(rows) if b not in edges]
+
+                @pl.when(phase == 0)
+                def _():
+                    for b in edges + inner:
+                        inbox[direction, 1, b + 1] = accum[0, b].astype(jnp.bfloat16)
                         each(sideways(direction, b), start)
 
-                    @pl.when(phase == 1)
-                    def _(b=b):
-                        finish(direction, b, jnp.where(is_thick, accum[b], first[b]), has_next)
+            ready = edges if last else [b for b in range(1, rows - 1) if position == len(groups) - 2]
+            if ready:
+
+                @pl.when(phase == 1)
+                def _(ready=ready):
+                    for b in ready:
+                        finish(direction, b, jnp.where(is_thick, accum[1, b], accum[0, b]), has_next)
 
     def one_direction(step, carry):
         direction = (own_first + step) % 2
@@ -268,8 +273,7 @@
             pltpu.VMEM((2, rows, height, width), jnp.float32),
             pltpu.VMEM((2, 2, rows + 2, height, width), jnp.bfloat16),
             pltpu.VMEM((height, (rows + 2) * depth), jnp.bfloat16),
-            pltpu.VMEM((rows, height, width), jnp.float32),
-            pltpu.VMEM((rows, height, width), jnp.float32),
+            pltpu.VMEM((2, rows, height, width), jnp.float32),
             pltpu.VMEM((2, rows, height, width), jnp.bfloat16),
             pltpu.SemaphoreType.DMA((2, rows, taps)),
             pltpu.SemaphoreType.DMA((2, rows)),
@@ -279,7 +283,7 @@
             pltpu.SemaphoreType.DMA((2, 2)),
         ],
         compiler_params=pltpu.CompilerParams(
-            collective_id=0, has_side_effects=True, vmem_limit_bytes=48 * 1024 * 1024
+            collective_id=0, has_side_effects=True, vmem_limit_bytes=60 * 1024 * 1024
         ),
         cost_estimate=pl.CostEstimate(
             flops=8 * rows * taps * height * depth * width,

time: 66.5 us -> 72.3 us (1.087)
  Pallas kernels: 62.8 us -> 69.6 us
  local copies, waits for them, and re-layouts: 2.87 us -> 1.87 us
    pallas_call x1, Pallas kernels: 62.8 us -> 69.6 us  [shards(): pl.pallas_call(functools.partial(sweep_kernel, layers, tiles, rows, width...]
    unnamed x5 -> x1, local copies, waits for them, and re-layouts: 2.87 us -> 1.87 us
where the time goes in v2:
time: 72.3 us; the launch traced here: 72.1 us
  Pallas kernels  69.6 us (96%)
  local copies, waits for them, and re-layouts  1.87 us (3%)
    pallas_call x1, Pallas kernels, shards(): pl.pallas_call(functools.partial(sweep_kernel, layers, tiles, rows, width...  69.6 us
    unnamed x1, local copies, waits for them, and re-layouts  1.87 us

profile of v2, /device:TPU:0, one launch (start us, length us, event | category | flops | bytes accessed | tf_op | source)
XLA Modules:
  0.0 72.1 jit_solution(987298120281173853)
XLA Ops:
  0.7 69.6 %shard_map.55 = f32[64,2048]{1,0:T(8,128)} custom-call(bf16[4,3072,512]{2,1,0:T(8,128)(2,1)} %bitcast.5, bf16[4,3072,512]{2,1,0:T(8,128)(2,1)} %bitcast.6, f32[64,2048]{1,0:T(8,128)} %bitcast.8, f32[64,2048]{1,0:T(8,128)} %bitcast.9, s32[1]{0:T(128)S(6)} %copy.7.thick_ref), custom_call_target="tpu_custom_call" | custom-call | flops 3221225472 | bytes 25165824 | tf_op jit(solution)/shard_map/pallas_call | solution.py:266
  70.2 1.9 %copy.8 = f32[1,2,32,2048]{3,2,1,0:T(8,128)} copy(f32[1,2,32,2048]{3,2,1,0:T(8,128)} %bitcast.7) | data formatting | bytes 1048576

commit v3 on v1

v3 whole, which is shorter than its diff:
```python
import functools

import jax
import jax.numpy as jnp
from jax import lax
from jax.experimental import pallas as pl
from jax.experimental.pallas import tpu as pltpu
from jax.sharding import PartitionSpec as P

MESH = pl.DeviceIdType.MESH
PHASES = 4


def sweep_kernel(
    layers, tiles, rows, width, cols,
    down_tiles, up_tiles, down_source, up_source, thick_ref, out_ref,
    weights, source, inbox, wide, accum, outbox, field, got, thick,
    tile_sem, tile_sent, source_sem, source_sent, recv_sem, next_sem, rim_sem, side_sem,
    field_sem, field_sent, thick_sem, thick_sent,
):
    layer = lax.axis_index("layer")
    tile = lax.axis_index("tile")
    pairs, strips = layers // 2, tiles * 2
    pair, core = layer // 2, layer % 2
    other = 1 - core
    strip = tile * 2 + core
    height = 2 * cols
    depth = 2 * width
    has_low, has_high = strip > 0, strip < strips - 1
    own_first = jnp.where(2 * pair < pairs, 0, 1)

    groups = [g for g in (list(range(2, rows)), sorted({1, rows}), [0, rows + 1]) if g]
    tile_order = [(b, j - b) for g in groups for j in g for b in range(rows) if 0 <= j - b <= 2]
    edges_first = sorted(range(rows), key=lambda b: 0 < b < rows - 1)

    def device(to_pair, to_strip):
        return {"layer": 2 * to_pair + to_strip % 2, "tile": to_strip // 2}

    partner = {"layer": 2 * pair + other, "tile": tile}

    def columns(part, b):
        return pl.ds(pl.multiple_of((part * rows + b) * width, width), width)

    def tile_here(ref, direction, par, b, k):
        taps = pl.ds(k * depth, depth)
        return pltpu.make_async_copy(
            ref.at[core * rows + b, taps], weights.at[direction, par, b, taps],
            tile_sem.at[direction, par, b, k],
        )

    def tile_there(ref, direction, par, b, k):
        taps = pl.ds(k * depth, depth)
        return pltpu.make_async_remote_copy(
            src_ref=ref.at[other * rows + b, taps], dst_ref=weights.at[direction, par, b, taps],
            send_sem=tile_sent.at[direction, b, k], recv_sem=tile_sem.at[direction, par, b, k],
            device_id=partner, device_id_type=MESH,
        )

    def source_here(ref, direction, par, b):
        return pltpu.make_async_copy(
            ref.at[:, columns(core, b)], source.at[direction, par, b], source_sem.at[direction, par, b]
        )

    def source_there(ref, direction, par, b):
        return pltpu.make_async_remote_copy(
            src_ref=ref.at[:, columns(other, b)], dst_ref=source.at[direction, par, b],
            send_sem=source_sent.at[direction, b], recv_sem=source_sem.at[direction, par, b],
            device_id=partner, device_id_type=MESH,
        )

    def thick_there(par):
        return pltpu.make_async_remote_copy(
            src_ref=thick.at[par], dst_ref=thick.at[par], send_sem=thick_sent, recv_sem=thick_sem,
            device_id=partner, device_id_type=MESH,
        )

    def field_there(par, b):
        return pltpu.make_async_remote_copy(
            src_ref=field.at[par, b], dst_ref=got.at[b], send_sem=field_sent.at[b],
            recv_sem=field_sem.at[b], device_id=partner, device_id_type=MESH,
        )

    tile_refs, source_refs = (down_tiles, up_tiles), (down_source, up_source)
    used = (layer > 0, layer < layers - 1)

    def tiles_in_order(what):
        for first in range(2):

            @pl.when(own_first == first)
            def _(first=first):
                for direction in (first, 1 - first):

                    @pl.when(used[direction])
                    def _(direction=direction):
                        for b, k in tile_order:
                            what(tile_refs[direction], direction, core, b, k)

    for direction in range(2):
        for b in range(rows):
            source_here(source_refs[direction], direction, core, b).start()
    tiles_in_order(lambda *at: tile_here(*at).start())

    barrier = pltpu.get_barrier_semaphore()
    met = 0
    for dp in (-1, 0, 1):
        for ds in (-1, 0, 1):
            if dp == 0 and ds == 0:
                continue
            there = (pair + dp >= 0) & (pair + dp < pairs) & (strip + ds >= 0) & (strip + ds < strips)

            @pl.when(there)
            def _(dp=dp, ds=ds):
                pl.semaphore_signal(
                    barrier, inc=1, device_id=device(pair + dp, strip + ds), device_id_type=MESH
                )

            met = met + jnp.where(there, 1, 0)

    field[...] = jnp.zeros_like(field)
    thick[core] = jnp.full((height, width), thick_ref[0], jnp.int32)
    no_trace = jnp.zeros((height, width), jnp.bfloat16)
    for absent, slot in ((jnp.logical_not(has_low), 0), (jnp.logical_not(has_high), rows + 1)):

        @pl.when(absent)
        def _(slot=slot):
            for direction in range(2):
                for phase in range(PHASES):
                    inbox[direction, phase, slot] = no_trace

    pl.semaphore_wait(barrier, met)
    for direction in range(2):
        for b in range(rows):
            source_there(source_refs[direction], direction, core, b).start()
    thick_there(core).start()
    tiles_in_order(lambda *at: tile_there(*at).start())

    def remote(src, direction, phase, slot, send_sem, to_pair, to_strip):
        return pltpu.make_async_remote_copy(
            src_ref=src, dst_ref=inbox.at[direction, phase, slot], send_sem=send_sem,
            recv_sem=recv_sem.at[direction, phase, slot],
            device_id=device(to_pair, to_strip), device_id_type=MESH,
        )

    def onward(direction, b):
        to_pair = pair + 1 - 2 * direction
        box = outbox.at[direction, b]
        copies = []
        if b == 0:
            copies.append((has_low, remote(
                box, direction, 0, rows + 1, rim_sem.at[direction, 0], to_pair, strip - 1)))
        if b == rows - 1:
            copies.append((has_high, remote(
                box, direction, 0, 0, rim_sem.at[direction, 1], to_pair, strip + 1)))
        copies.append((None, remote(
            box, direction, 0, b + 1, next_sem.at[direction, b], to_pair, strip)))
        return copies

    def sideways(direction, phase, b):
        box = inbox.at[direction, phase + 1, b + 1]
        copies = []
        if b == 0:
            copies.append((has_low, remote(
                box, direction, phase + 1, rows + 1, side_sem.at[direction, phase, 0], pair, strip - 1)))
        if b == rows - 1:
            copies.append((has_high, remote(
                box, direction, phase + 1, 0, side_sem.at[direction, phase, 1], pair, strip + 1)))
        return copies

    def each(copies, what):
        for condition, copy in copies:
            if condition is None:
                what(copy)
            else:
                pl.when(condition)(functools.partial(what, copy))

    def start(copy):
        copy.start()

    def sent(copy):
        copy.wait_send()

    def arrived(direction, phase, slot):
        def wait():
            remote(
                inbox.at[direction, phase, slot], direction, phase, slot,
                next_sem.at[direction, 0], pair, strip,
            ).wait_recv()

        if slot == 0:
            pl.when(has_low)(wait)
        elif slot == rows + 1:
            pl.when(has_high)(wait)
        else:
            pl.when(phase == 0)(wait)

    def passed(direction, phase, b, value):
        inbox[direction, phase + 1, b + 1] = value.astype(jnp.bfloat16)
        each(sideways(direction, phase, b), start)

    def finish(step, direction, phase, par, b, moved, has_next):
        @pl.when(par == core)
        def _():
            source_here(down_source, direction, par, b).wait()

        @pl.when(par == other)
        def _():
            source_there(down_source, direction, par, b).wait_recv()

        value = source[direction, par, b]
        if moved is not None:
            value = value + moved
            accum[0, b] = value

            @pl.when((phase == PHASES - 1) & has_next)
            def _():
                outbox[direction, b] = accum[0, b].astype(jnp.bfloat16)
                each(onward(direction, b), start)

            @pl.when(phase < PHASES - 1)
            def _():
                passed(direction, phase, b, accum[0, b])

        else:
            passed(direction, phase, b, value)
        field[par, b] += value

        @pl.when((step == 1) & (par == other))
        def _():
            field_there(par, b).start()

        @pl.when((step == 1) & (par == core))
        def _():
            out_ref[:, columns(core, b)] = field[par, b]

    def one_phase(step, phase, direction, has_next):
        touched = set()
        done = 0
        half, odd = phase // 2, phase % 2
        par = jnp.where(direction == 0, half, 1 - half)
        for group in groups:
            for j in group:
                arrived(direction, phase, j)
                x = inbox[direction, phase, j]
                wide[:, pl.ds(j * depth, width)] = x
                wide[:, pl.ds(j * depth + width, width)] = jnp.concatenate([-x[cols:], x[:cols]], axis=0)
            for b in range(rows):
                taps = [j - b for j in group if 0 <= j - b <= 2]
                if not taps:
                    continue

                @pl.when((odd == 0) & (par == core))
                def _(b=b, taps=taps):
                    for k in taps:
                        tile_here(down_tiles, direction, par, b, k).wait()

                @pl.when((odd == 0) & (par == other))
                def _(b=b, taps=taps):
                    for k in taps:
                        tile_there(down_tiles, direction, par, b, k).wait_recv()

                runs = []
                for k in taps:
                    if runs and runs[-1][1] == k:
                        runs[-1][1] = k + 1
                    else:
                        runs.append([k, k + 1])
                total = None
                for low, high in runs:
                    part = jnp.dot(
                        wide[:, pl.ds((b + low) * depth, (high - low) * depth)],
                        weights[direction, par, b, pl.ds(low * depth, (high - low) * depth)],
                        preferred_element_type=jnp.float32,
                    )
                    total = part if total is None else total + part
                accum[odd, b] = accum[odd, b] + total if b in touched else total
                touched.add(b)
                done |= sum(1 << (3 * b + k) for k in taps)
                if (done >> (3 * b)) & 7 == 7:

                    @pl.when(odd == 0)
                    def _(b=b):
                        passed(direction, phase, b, accum[0, b])

                    @pl.when(odd == 1)
                    def _(b=b):
                        moved = jnp.where(thick[par] == 2, accum[1, b], accum[0, b])
                        finish(step, direction, phase, par, b, moved, has_next)

    def one_direction(step, carry):
        direction = (own_first + step) % 2
        begins = jnp.where(direction == 0, pair == 0, pair == pairs - 1)
        has_next = jnp.where(direction == 0, pair < pairs - 1, pair > 0)

        @pl.when(begins)
        def _():
            for b in edges_first:
                finish(step, direction, 1, direction, b, None, has_next)

        @pl.when(step == 0)
        def _():
            thick_there(other).wait_recv()

        def body(phase, inner):
            one_phase(step, phase, direction, has_next)
            return inner

        lax.fori_loop(jnp.where(begins, 2, 0), PHASES, body, 0)

        def drain(phase, inner):
            for b in range(rows):
                each(sideways(direction, phase, b), sent)
            return inner

        lax.fori_loop(jnp.where(begins, 1, 0), PHASES - 1, drain, 0)
        return carry

    lax.fori_loop(0, 2, one_direction, 0)

    for direction in range(2):
        for b in range(rows):
            source_there(source_refs[direction], direction, core, b).wait_send()
    thick_there(core).wait_send()
    tiles_in_order(lambda *at: tile_there(*at).wait_send())
    for direction in range(2):

        @pl.when(pair < pairs - 1 if direction == 0 else pair > 0)
        def _(direction=direction):
            for b in range(rows):
                each(onward(direction, b), sent)

    for b in range(rows):
        field_there(other, b).wait_recv()
        out_ref[:, columns(other, b)] = got[b]
    for b in range(rows):
        field_there(other, b).wait_send()


def shards(layers, tiles, down_tiles, up_tiles, down_source, up_source, thickness):
    _, blocks, taps, parts, width, _ = down_tiles.shape
    cols = down_source.shape[2]
    rows = blocks // 2
    height, depth = parts * cols, parts * width
    flat_tiles = (blocks, taps * depth, width)
    flat = (height, blocks * width)
    anywhere = pl.BlockSpec(memory_space=pl.ANY)
    dma = pltpu.SemaphoreType.DMA
    field = pl.pallas_call(
        functools.partial(sweep_kernel, layers, tiles, rows, width, cols),
        out_shape=jax.ShapeDtypeStruct(flat, jnp.float32),
        in_specs=[anywhere] * 4 + [pl.BlockSpec(memory_space=pltpu.SMEM)],
        out_specs=pl.BlockSpec(memory_space=pltpu.VMEM),
        scratch_shapes=[
            pltpu.VMEM((2, 2, rows, taps * depth, width), jnp.bfloat16),
            pltpu.VMEM((2, 2, rows, height, width), jnp.float32),
            pltpu.VMEM((2, PHASES, rows + 2, height, width), jnp.bfloat16),
            pltpu.VMEM((height, (rows + 2) * depth), jnp.bfloat16),
            pltpu.VMEM((2, rows, height, width), jnp.float32),
            pltpu.VMEM((2, rows, height, width), jnp.bfloat16),
            pltpu.VMEM((2, rows, height, width), jnp.float32),
            pltpu.VMEM((rows, height, width), jnp.float32),
            pltpu.VMEM((2, height, width), jnp.int32),
            dma((2, 2, rows, taps)),
            dma((2, rows, taps)),
            dma((2, 2, rows)),
            dma((2, rows)),
            dma((2, PHASES, rows + 2)),
            dma((2, rows)),
            dma((2, 2)),
            dma((2, PHASES - 1, 2)),
            dma((rows,)),
            dma((rows,)),
            dma,
            dma,
        ],
        compiler_params=pltpu.CompilerParams(
            collective_id=0, has_side_effects=True, vmem_limit_bytes=60 * 1024 * 1024
        ),
        cost_estimate=pl.CostEstimate(
            flops=16 * rows * taps * height * depth * width,
            bytes_accessed=8 * rows * taps * depth * width,
            transcendentals=0,
        ),
    )(
        down_tiles.reshape(flat_tiles),
        up_tiles.reshape(flat_tiles),
        down_source.reshape(flat),
        up_source.reshape(flat),
        thickness,
    )
    return field.reshape(down_source.shape)


def solution(mesh):
    return jax.shard_map(
        functools.partial(shards, mesh.shape["layer"], mesh.shape["tile"]),
        mesh=mesh,
        in_specs=(
            P("layer", "tile", None, None, None, None),
            P("layer", "tile", None, None, None, None),
            P("layer", None, None, "tile"),
            P("layer", None, None, "tile"),
            P("layer"),
        ),
        out_specs=P("layer", None, None, "tile"),
        check_vma=False,
    )
```

time: 66.5 us -> 76.6 us (1.15)
  Pallas kernels: 62.8 us -> 73.4 us
  local copies, waits for them, and re-layouts: 2.87 us -> 1.87 us
    pallas_call x1, Pallas kernels: 62.8 us -> 73.4 us  [shards(): pl.pallas_call(functools.partial(sweep_kernel, layers, tiles, rows, width...]
    unnamed x5 -> x1, local copies, waits for them, and re-layouts: 2.87 us -> 1.87 us
where the time goes in v3:
time: 76.6 us; the launch traced here: 75.9 us
  Pallas kernels  73.4 us (96%)
  local copies, waits for them, and re-layouts  1.87 us (2%)
    pallas_call x1, Pallas kernels, shards(): pl.pallas_call(functools.partial(sweep_kernel, layers, tiles, rows, width...  73.4 us
    unnamed x1, local copies, waits for them, and re-layouts  1.87 us

profile of v3, /device:TPU:0, one launch (start us, length us, event | category | flops | bytes accessed | tf_op | source)
XLA Modules:
  0.0 75.9 jit_solution(14811039523614470616)
XLA Ops:
  0.7 73.4 %shard_map.55 = f32[64,2048]{1,0:T(8,128)} custom-call(bf16[4,3072,512]{2,1,0:T(8,128)(2,1)} %bitcast.5, bf16[4,3072,512]{2,1,0:T(8,128)(2,1)} %bitcast.6, f32[64,2048]{1,0:T(8,128)} %bitcast.8, f32[64,2048]{1,0:T(8,128)} %bitcast.9, s32[1]{0:T(128)S(6)} %copy.7.thick_ref), custom_call_target="tpu_custom_call" | custom-call | flops 3221225472 | bytes 25165824 | tf_op jit(solution)/shard_map/pallas_call | solution.py:347
  74.1 1.9 %copy.8 = f32[1,2,32,2048]{3,2,1,0:T(8,128)} copy(f32[1,2,32,2048]{3,2,1,0:T(8,128)} %bitcast.7) | data formatting | bytes 1048576

commit v4 on v3

v4 whole, which is shorter than its diff:
```python
import functools

import jax
import jax.numpy as jnp
from jax import lax
from jax.experimental import pallas as pl
from jax.experimental.pallas import tpu as pltpu
from jax.sharding import PartitionSpec as P

MESH = pl.DeviceIdType.MESH
PHASES = 4


def sweep_kernel(
    layers, tiles, rows, width, cols,
    down_tiles, up_tiles, down_source, up_source, thick_ref, out_ref,
    weights, source, inbox, wide, accum, outbox, field, got, thick,
    tile_sem, tile_sent, source_sem, source_sent, recv_sem, next_sem, rim_sem, side_sem,
    field_sem, field_sent, thick_sem, thick_sent,
):
    layer = lax.axis_index("layer")
    tile = lax.axis_index("tile")
    pairs, strips = layers // 2, tiles * 2
    pair, core = layer // 2, layer % 2
    other = 1 - core
    strip = tile * 2 + core
    height = 2 * cols
    depth = 2 * width
    has_low, has_high = strip > 0, strip < strips - 1
    own_first = jnp.where(2 * pair < pairs, 0, 1)

    products = 3 * rows

    def loop(low, high, what):
        def body(index, carry):
            what(index)
            return carry

        lax.fori_loop(low, high, body, 0)

    def device(to_pair, to_strip):
        return {"layer": 2 * to_pair + to_strip % 2, "tile": to_strip // 2}

    partner = {"layer": 2 * pair + other, "tile": tile}

    def columns(part, b):
        return pl.ds(pl.multiple_of((part * rows + b) * width, width), width)

    def tile_here(ref, direction, par, b, k):
        taps = pl.ds(pl.multiple_of(k * depth, depth), depth)
        return pltpu.make_async_copy(
            ref.at[core * rows + b, taps], weights.at[direction, par, b, taps],
            tile_sem.at[direction, par, b, k],
        )

    def tile_there(ref, direction, par, b, k):
        taps = pl.ds(pl.multiple_of(k * depth, depth), depth)
        return pltpu.make_async_remote_copy(
            src_ref=ref.at[other * rows + b, taps], dst_ref=weights.at[direction, par, b, taps],
            send_sem=tile_sent.at[direction, b, k], recv_sem=tile_sem.at[direction, par, b, k],
            device_id=partner, device_id_type=MESH,
        )

    def source_here(ref, direction, par, b):
        return pltpu.make_async_copy(
            ref.at[:, columns(core, b)], source.at[direction, par, b], source_sem.at[direction, par, b]
        )

    def source_there(ref, direction, par, b):
        return pltpu.make_async_remote_copy(
            src_ref=ref.at[:, columns(other, b)], dst_ref=source.at[direction, par, b],
            send_sem=source_sent.at[direction, b], recv_sem=source_sem.at[direction, par, b],
            device_id=partner, device_id_type=MESH,
        )

    def thick_there(par):
        return pltpu.make_async_remote_copy(
            src_ref=thick.at[par], dst_ref=thick.at[par], send_sem=thick_sent, recv_sem=thick_sem,
            device_id=partner, device_id_type=MESH,
        )

    def field_there(par, b):
        return pltpu.make_async_remote_copy(
            src_ref=field.at[par, b], dst_ref=got.at[b], send_sem=field_sent.at[b],
            recv_sem=field_sem.at[b], device_id=partner, device_id_type=MESH,
        )

    refs = ((down_tiles, down_source), (up_tiles, up_source))
    used = (layer > 0, layer < layers - 1)

    def each_direction(what):
        def one(step):
            chosen = (own_first + step) % 2
            for direction in range(2):
                pl.when(chosen == direction)(functools.partial(what, direction))

        loop(0, 2, one)

    def loads(direction, of_tile, of_source):
        tiles_ref, source_ref = refs[direction]
        loop(0, rows, lambda b: of_source(source_ref, direction, core, b))

        @pl.when(used[direction])
        def _():
            loop(1, products - 1, lambda i: of_tile(tiles_ref, direction, core, i // 3, i % 3))
            for i in (0, products - 1):
                of_tile(tiles_ref, direction, core, i // 3, i % 3)

    each_direction(lambda direction: loads(
        direction, lambda *at: tile_here(*at).start(), lambda *at: source_here(*at).start()))

    barrier = pltpu.get_barrier_semaphore()
    met = 0
    for dp in (-1, 0, 1):
        for ds in (-1, 0, 1):
            if dp == 0 and ds == 0:
                continue
            there = (pair + dp >= 0) & (pair + dp < pairs) & (strip + ds >= 0) & (strip + ds < strips)

            @pl.when(there)
            def _(dp=dp, ds=ds):
                pl.semaphore_signal(
                    barrier, inc=1, device_id=device(pair + dp, strip + ds), device_id_type=MESH
                )

            met = met + jnp.where(there, 1, 0)

    field[...] = jnp.zeros_like(field)
    thick[core] = jnp.full((height, width), thick_ref[0], jnp.int32)
    no_trace = jnp.zeros((height, width), jnp.bfloat16)
    for absent, slot in ((jnp.logical_not(has_low), 0), (jnp.logical_not(has_high), rows + 1)):

        @pl.when(absent)
        def _(slot=slot):
            for direction in range(2):
                for phase in range(PHASES):
                    inbox[direction, phase, slot] = no_trace

    pl.semaphore_wait(barrier, met)
    thick_there(core).start()
    each_direction(lambda direction: loads(
        direction, lambda *at: tile_there(*at).start(), lambda *at: source_there(*at).start()))

    def remote(src, direction, phase, slot, send_sem, to_pair, to_strip):
        return pltpu.make_async_remote_copy(
            src_ref=src, dst_ref=inbox.at[direction, phase, slot], send_sem=send_sem,
            recv_sem=recv_sem.at[direction, phase, slot],
            device_id=device(to_pair, to_strip), device_id_type=MESH,
        )

    def onward(direction, b):
        return remote(
            outbox.at[direction, b], direction, 0, b + 1, next_sem.at[direction, b],
            pair + 1 - 2 * direction, strip)

    def rim(direction, side):
        return remote(
            outbox.at[direction, side * (rows - 1)], direction, 0, (1 - side) * (rows + 1),
            rim_sem.at[direction, side], pair + 1 - 2 * direction, strip + 2 * side - 1)

    def sideways(direction, phase, side):
        return remote(
            inbox.at[direction, phase + 1, 1 + side * (rows - 1)], direction, phase + 1,
            (1 - side) * (rows + 1), side_sem.at[direction, phase, side], pair, strip + 2 * side - 1)

    def has(side):
        return jnp.where(side == 0, has_low, has_high)

    def arrived(direction, phase, slot):
        remote(
            inbox.at[direction, phase, slot], direction, phase, slot,
            next_sem.at[direction, 0], pair, strip,
        ).wait_recv()

    def passed(direction, phase, b, sides):
        inbox[direction, phase + 1, b + 1] = accum[0, b].astype(jnp.bfloat16)
        for side in sides:
            pl.when(has(side))(lambda side=side: sideways(direction, phase, side).start())

    def finish(step, direction, phase, par, b, moved, sides, has_next):
        @pl.when(par == core)
        def _():
            source_here(down_source, direction, par, b).wait()

        @pl.when(par == other)
        def _():
            source_there(down_source, direction, par, b).wait_recv()

        value = source[direction, par, b] + moved if moved is not None else source[direction, par, b]
        accum[0, b] = value

        @pl.when((phase == PHASES - 1) & has_next)
        def _():
            outbox[direction, b] = accum[0, b].astype(jnp.bfloat16)
            for side in sides:
                pl.when(has(side))(lambda side=side: rim(direction, side).start())
            onward(direction, b).start()

        @pl.when(phase < PHASES - 1)
        def _():
            passed(direction, phase, b, sides)

        field[par, b] += accum[0, b]

        @pl.when((step == 1) & (par == other))
        def _():
            field_there(par, b).start()

        @pl.when((step == 1) & (par == core))
        def _():
            out_ref[:, columns(core, b)] = field[par, b]

    def widen(direction, phase, slot):
        x = inbox[direction, phase, slot]
        wide[slot, :, pl.ds(0, width)] = x
        wide[slot, :, pl.ds(width, width)] = jnp.concatenate([-x[cols:], x[:cols]], axis=0)

    def product(direction, par, odd, b, k):
        @pl.when((odd == 0) & (par == core))
        def _():
            tile_here(down_tiles, direction, par, b, k).wait()

        @pl.when((odd == 0) & (par == other))
        def _():
            tile_there(down_tiles, direction, par, b, k).wait_recv()

        accum[odd, b] += jnp.dot(
            wide[b + k], weights[direction, par, b, pl.ds(pl.multiple_of(k * depth, depth), depth)],
            preferred_element_type=jnp.float32,
        )

    def one_phase(step, phase, direction, has_next):
        half, odd = phase // 2, phase % 2
        par = jnp.where(direction == 0, half, 1 - half)

        def own_input(b):
            pl.when(phase == 0)(lambda: arrived(direction, phase, b + 1))
            widen(direction, phase, b + 1)
            accum[odd, b] = jnp.zeros((height, width), jnp.float32)

        loop(0, rows, own_input)
        loop(1, products - 1, lambda i: product(direction, par, odd, i // 3, i % 3))

        def complete(b, sides):
            @pl.when(odd == 0)
            def _():
                passed(direction, phase, b, sides)

            @pl.when(odd == 1)
            def _():
                moved = jnp.where(thick[par] == 2, accum[1, b], accum[0, b])
                finish(step, direction, phase, par, b, moved, sides, has_next)

        def rim_input(index):
            side = (1 - core + index) % 2
            slot, b = side * (rows + 1), side * (rows - 1)
            pl.when(has(side))(lambda: arrived(direction, phase, slot))
            widen(direction, phase, slot)
            product(direction, par, odd, b, 2 * side)
            if rows > 1:
                complete(b, [side])

        loop(0, 2, rim_input)
        if rows == 1:
            complete(0, [0, 1])
        elif rows > 2:
            loop(1, rows - 1, lambda b: complete(b, []))

    def one_direction(step, carry):
        direction = (own_first + step) % 2
        begins = jnp.where(direction == 0, pair == 0, pair == pairs - 1)
        has_next = jnp.where(direction == 0, pair < pairs - 1, pair > 0)

        @pl.when(begins)
        def _():
            for b in range(rows):
                sides = [side for side in range(2) if b == side * (rows - 1)]
                finish(step, direction, 1, direction, b, None, sides, has_next)

        @pl.when(step == 0)
        def _():
            thick_there(other).wait_recv()

        def body(phase, inner):
            one_phase(step, phase, direction, has_next)
            return inner

        lax.fori_loop(jnp.where(begins, 2, 0), PHASES, body, 0)

        def drain(phase, inner):
            for side in range(2):
                pl.when(has(side))(lambda side=side: sideways(direction, phase, side).wait_send())
            return inner

        lax.fori_loop(jnp.where(begins, 1, 0), PHASES - 1, drain, 0)

        @pl.when(has_next)
        def _():
            loop(0, rows, lambda b: onward(direction, b).wait_send())
            for side in range(2):
                pl.when(has(side))(lambda side=side: rim(direction, side).wait_send())

        return carry

    lax.fori_loop(0, 2, one_direction, 0)

    thick_there(core).wait_send()
    each_direction(lambda direction: loads(
        direction, lambda *at: tile_there(*at).wait_send(), lambda *at: source_there(*at).wait_send()))

    for b in range(rows):
        field_there(other, b).wait_recv()
        out_ref[:, columns(other, b)] = got[b]
    for b in range(rows):
        field_there(other, b).wait_send()


def shards(layers, tiles, down_tiles, up_tiles, down_source, up_source, thickness):
    _, blocks, taps, parts, width, _ = down_tiles.shape
    cols = down_source.shape[2]
    rows = blocks // 2
    height, depth = parts * cols, parts * width
    flat_tiles = (blocks, taps * depth, width)
    flat = (height, blocks * width)
    anywhere = pl.BlockSpec(memory_space=pl.ANY)
    dma = pltpu.SemaphoreType.DMA
    field = pl.pallas_call(
        functools.partial(sweep_kernel, layers, tiles, rows, width, cols),
        out_shape=jax.ShapeDtypeStruct(flat, jnp.float32),
        in_specs=[anywhere] * 4 + [pl.BlockSpec(memory_space=pltpu.SMEM)],
        out_specs=pl.BlockSpec(memory_space=pltpu.VMEM),
        scratch_shapes=[
            pltpu.VMEM((2, 2, rows, taps * depth, width), jnp.bfloat16),
            pltpu.VMEM((2, 2, rows, height, width), jnp.float32),
            pltpu.VMEM((2, PHASES, rows + 2, height, width), jnp.bfloat16),
            pltpu.VMEM((rows + 2, height, depth), jnp.bfloat16),
            pltpu.VMEM((2, rows, height, width), jnp.float32),
            pltpu.VMEM((2, rows, height, width), jnp.bfloat16),
            pltpu.VMEM((2, rows, height, width), jnp.float32),
            pltpu.VMEM((rows, height, width), jnp.float32),
            pltpu.VMEM((2, height, width), jnp.int32),
            dma((2, 2, rows, taps)),
            dma((2, rows, taps)),
            dma((2, 2, rows)),
            dma((2, rows)),
            dma((2, PHASES, rows + 2)),
            dma((2, rows)),
            dma((2, 2)),
            dma((2, PHASES - 1, 2)),
            dma((rows,)),
            dma((rows,)),
            dma,
            dma,
        ],
        compiler_params=pltpu.CompilerParams(
            collective_id=0, has_side_effects=True, vmem_limit_bytes=60 * 1024 * 1024
        ),
        cost_estimate=pl.CostEstimate(
            flops=16 * rows * taps * height * depth * width,
            bytes_accessed=8 * rows * taps * depth * width,
            transcendentals=0,
        ),
    )(
        down_tiles.reshape(flat_tiles),
        up_tiles.reshape(flat_tiles),
        down_source.reshape(flat),
        up_source.reshape(flat),
        thickness,
    )
    return field.reshape(down_source.shape)


def solution(mesh):
    return jax.shard_map(
        functools.partial(shards, mesh.shape["layer"], mesh.shape["tile"]),
        mesh=mesh,
        in_specs=(
            P("layer", "tile", None, None, None, None),
            P("layer", "tile", None, None, None, None),
            P("layer", None, None, "tile"),
            P("layer", None, None, "tile"),
            P("layer"),
        ),
        out_specs=P("layer", None, None, "tile"),
        check_vma=False,
    )
```

time: 76.6 us -> 76.9 us (level)
  Pallas kernels: 73.4 us -> 74.2 us
where the time goes in v4:
time: 76.9 us; the launch traced here: 76.7 us
  Pallas kernels  74.2 us (96%)
  local copies, waits for them, and re-layouts  1.87 us (2%)
    pallas_call x1, Pallas kernels, shards(): pl.pallas_call(functools.partial(sweep_kernel, layers, tiles, rows, width...  74.2 us
    unnamed x1, local copies, waits for them, and re-layouts  1.87 us

profile of v4, /device:TPU:0, one launch (start us, length us, event | category | flops | bytes accessed | tf_op | source)
XLA Modules:
  0.0 76.7 jit_solution(13525309248162054970)
XLA Ops:
  0.7 74.2 %shard_map.55 = f32[64,2048]{1,0:T(8,128)} custom-call(bf16[4,3072,512]{2,1,0:T(8,128)(2,1)} %bitcast.5, bf16[4,3072,512]{2,1,0:T(8,128)(2,1)} %bitcast.6, f32[64,2048]{1,0:T(8,128)} %bitcast.8, f32[64,2048]{1,0:T(8,128)} %bitcast.9, s32[1]{0:T(128)S(6)} %copy.7.thick_ref), custom_call_target="tpu_custom_call" | custom-call | flops 3221225472 | bytes 25165824 | tf_op jit(solution)/shard_map/pallas_call | solution.py:327
  74.8 1.9 %copy.8 = f32[1,2,32,2048]{3,2,1,0:T(8,128)} copy(f32[1,2,32,2048]{3,2,1,0:T(8,128)} %bitcast.7) | data formatting | bytes 1048576

commit v5 on v1

--- a/solution.py
+++ b/solution.py
@@ -24,7 +24,7 @@
     has_low, has_high = tile > 0, tile < tiles - 1
     own_first = jnp.where(2 * layer < layers, 0, 1)
 
-    groups = [g for g in (list(range(2, rows)), sorted({1, rows}), [0, rows + 1]) if g]
+    groups = [g for g in (list(range(2, rows)), sorted({1, rows}), [0], [rows + 1]) if g]
 
     def tile_copy(ref, direction, b, k):
         return pltpu.make_async_copy(
@@ -92,10 +92,16 @@
     pl.semaphore_wait(barrier, met)
     is_thick = jnp.full((height, width), thick_ref[0], jnp.int32) == 2
 
-    def remote(src, direction, phase, slot, send_sem, to_layer, to_tile):
+    pieces = height // 16 if height % 16 == 0 else 1
+
+    def remote(src, direction, phase, slot, send_sem, to_layer, to_tile, piece=None):
+        dst = inbox.at[direction, phase, slot]
+        if piece is not None:
+            span = pl.ds(piece * (height // pieces), height // pieces)
+            src, dst = src.at[span], dst.at[span]
         return pltpu.make_async_remote_copy(
             src_ref=src,
-            dst_ref=inbox.at[direction, phase, slot],
+            dst_ref=dst,
             send_sem=send_sem,
             recv_sem=recv_sem.at[direction, phase, slot],
             device_id={"layer": to_layer, "tile": to_tile},
@@ -107,24 +113,24 @@
         box = outbox.at[direction, b]
         copies = []
         if b == 0:
-            copies.append((has_low, remote(
-                box, direction, 0, rows + 1, rim_sem.at[direction, 0], to_layer, tile - 1)))
+            copies.append((has_low, functools.partial(
+                remote, box, direction, 0, rows + 1, rim_sem.at[direction, 0], to_layer, tile - 1)))
         if b == rows - 1:
-            copies.append((has_high, remote(
-                box, direction, 0, 0, rim_sem.at[direction, 1], to_layer, tile + 1)))
-        copies.append((None, remote(
-            box, direction, 0, b + 1, next_sem.at[direction, b], to_layer, tile)))
+            copies.append((has_high, functools.partial(
+                remote, box, direction, 0, 0, rim_sem.at[direction, 1], to_layer, tile + 1)))
+        copies.append((None, functools.partial(
+            remote, box, direction, 0, b + 1, next_sem.at[direction, b], to_layer, tile)))
         return copies
 
     def sideways(direction, b):
         box = inbox.at[direction, 1, b + 1]
         copies = []
         if b == 0:
-            copies.append((has_low, remote(
-                box, direction, 1, rows + 1, mid_sem.at[direction, 0], layer, tile - 1)))
+            copies.append((has_low, functools.partial(
+                remote, box, direction, 1, rows + 1, mid_sem.at[direction, 0], layer, tile - 1)))
         if b == rows - 1:
-            copies.append((has_high, remote(
-                box, direction, 1, 0, mid_sem.at[direction, 1], layer, tile + 1)))
+            copies.append((has_high, functools.partial(
+                remote, box, direction, 1, 0, mid_sem.at[direction, 1], layer, tile + 1)))
         return copies
 
     def each(copies, what):
@@ -135,10 +141,11 @@
                 pl.when(condition)(functools.partial(what, copy))
 
     def start(copy):
-        copy.start()
+        for piece in range(pieces):
+            copy(piece=piece).start()
 
     def sent(copy):
-        copy.wait_send()
+        copy().wait_send()
 
     def arrived(direction, phase, slot):
         def wait():
@@ -160,12 +167,13 @@
         value = source[direction, b]
         if moved is not None:
             value = value + moved
-        out_ref[:, columns] += value
 
         @pl.when(has_next)
         def _():
             outbox[direction, b] = value.astype(jnp.bfloat16)
             each(onward(direction, b), start)
+
+        out_ref[:, columns] += value
 
     def one_phase(phase, direction, has_next):
         touched = set()
@@ -208,9 +216,9 @@
 
                     @pl.when(phase == 0)
                     def _(b=b):
-                        first[b] = accum[b]
                         inbox[direction, 1, b + 1] = accum[b].astype(jnp.bfloat16)
                         each(sideways(direction, b), start)
+                        first[b] = accum[b]
 
                     @pl.when(phase == 1)
                     def _(b=b):

time: 66.5 us -> 64.8 us (0.974)
  Pallas kernels: 62.8 us -> 61 us
    pallas_call x1, Pallas kernels: 62.8 us -> 61 us  [shards(): pl.pallas_call(functools.partial(sweep_kernel, layers, tiles, rows, width...]
where the time goes in v5:
time: 64.8 us; the launch traced here: 64.6 us
  Pallas kernels  61 us (94%)
  local copies, waits for them, and re-layouts  2.87 us (4%)
  between operations  0.67 us (1%)
    pallas_call x1, Pallas kernels, shards(): pl.pallas_call(functools.partial(sweep_kernel, layers, tiles, rows, width...  61 us
    unnamed x5, local copies, waits for them, and re-layouts  2.87 us

profile of v5, /device:TPU:0, one launch (start us, length us, event | category | flops | bytes accessed | tf_op | source)
XLA Modules:
  0.0 64.6 jit_solution(5449012615420022250)
XLA Ops:
  0.7 0.0 copy-start
  0.7 1.0 %copy-done = f32[1,2,32,2048]{3,2,1,0:T(8,128)S(1)} copy-done((f32[1,2,32,2048]{3,2,1,0:T(8,128)S(1)}, f32[1,2,32,2048]{3,2,1,0:T(8,128)}, u32[]{:S(2)}) %copy-start) | copy-done | bytes 524312
  1.7 0.0 copy-start.1
  1.7 1.0 %copy-done.1 = f32[1,2,32,2048]{3,2,1,0:T(8,128)S(1)} copy-done((f32[1,2,32,2048]{3,2,1,0:T(8,128)S(1)}, f32[1,2,32,2048]{3,2,1,0:T(8,128)}, u32[]{:S(2)}) %copy-start.1) | copy-done | bytes 524312
  2.7 61.0 %shard_map.55 = f32[64,2048]{1,0:T(8,128)S(1)} custom-call(bf16[4,3072,512]{2,1,0:T(8,128)(2,1)} %bitcast.8, bf16[4,3072,512]{2,1,0:T(8,128)(2,1)} %bitcast.9, f32[64,2048]{1,0:T(8,128)S(1)} %bitcast.6, f32[64,2048]{1,0:T(8,128)S(1)} %bitcast.7, s32[1]{0:T(128)S(6)} %copy.7.thick_ref), custom_call_target="tpu_custom_call" | custom-call | flops 3221225472 | bytes 25165824 | tf_op jit(solution)/shard_map/pallas_call | solution.py:269
  63.8 0.8 %copy.8 = f32[1,2,32,2048]{3,2,1,0:T(8,128)} copy(f32[1,2,32,2048]{3,2,1,0:T(8,128)S(1)} %bitcast.5) | data formatting | bytes 1048576
Async XLA Ops:
  0.7 1.0 %copy-start = (f32[1,2,32,2048]{3,2,1,0:T(8,128)S(1)}, f32[1,2,32,2048]{3,2,1,0:T(8,128)}, u32[]{:S(2)}) copy-start(f32[1,2,32,2048]{3,2,1,0:T(8,128)} %param.7) | copy-start | bytes 1572868
  1.7 1.0 %copy-start.1 = (f32[1,2,32,2048]{3,2,1,0:T(8,128)S(1)}, f32[1,2,32,2048]{3,2,1,0:T(8,128)}, u32[]{:S(2)}) copy-start(f32[1,2,32,2048]{3,2,1,0:T(8,128)} %param.8) | copy-start | bytes 1572868

commit v6 on v5

--- a/solution.py
+++ b/solution.py
@@ -287,7 +287,7 @@
             pltpu.SemaphoreType.DMA((2, 2)),
         ],
         compiler_params=pltpu.CompilerParams(
-            collective_id=0, has_side_effects=True, vmem_limit_bytes=48 * 1024 * 1024
+            collective_id=0, has_side_effects=True, vmem_limit_bytes=60 * 1024 * 1024
         ),
         cost_estimate=pl.CostEstimate(
             flops=8 * rows * taps * height * depth * width,

time: 64.8 us -> 70.5 us (1.088)
  Pallas kernels: 61 us -> 67.8 us
  local copies, waits for them, and re-layouts: 2.87 us -> 1.87 us
    pallas_call x1, Pallas kernels: 61 us -> 67.8 us  [shards(): pl.pallas_call(functools.partial(sweep_kernel, layers, tiles, rows, width...]
    unnamed x5 -> x1, local copies, waits for them, and re-layouts: 2.87 us -> 1.87 us
where the time goes in v6:
time: 70.5 us; the launch traced here: 70.3 us
  Pallas kernels  67.8 us (96%)
  local copies, waits for them, and re-layouts  1.87 us (3%)
    pallas_call x1, Pallas kernels, shards(): pl.pallas_call(functools.partial(sweep_kernel, layers, tiles, rows, width...  67.8 us
    unnamed x1, local copies, waits for them, and re-layouts  1.87 us

profile of v6, /device:TPU:0, one launch (start us, length us, event | category | flops | bytes accessed | tf_op | source)
XLA Modules:
  0.0 70.3 jit_solution(13967616353660875313)
XLA Ops:
  0.7 67.8 %shard_map.55 = f32[64,2048]{1,0:T(8,128)} custom-call(bf16[4,3072,512]{2,1,0:T(8,128)(2,1)} %bitcast.5, bf16[4,3072,512]{2,1,0:T(8,128)(2,1)} %bitcast.6, f32[64,2048]{1,0:T(8,128)} %bitcast.8, f32[64,2048]{1,0:T(8,128)} %bitcast.9, s32[1]{0:T(128)S(6)} %copy.7.thick_ref), custom_call_target="tpu_custom_call" | custom-call | flops 3221225472 | bytes 25165824 | tf_op jit(solution)/shard_map/pallas_call | solution.py:269
  68.4 1.9 %copy.8 = f32[1,2,32,2048]{3,2,1,0:T(8,128)} copy(f32[1,2,32,2048]{3,2,1,0:T(8,128)} %bitcast.7) | data formatting | bytes 1048576
